TPU v7x, 256 devices: a whole 4x4x8 slice. The times are simulated.
256 devices in a mesh: row: 32 (over x, y, z_hi), col: 8 (over z_lo, core).
Axes of the slice: x: 4, y: 4, z: 8 (z_hi: 2, z_lo: 4; z = z_hi * 4 + z_lo), core: 2. Of those that a mesh axis runs over, the one named last changes fastest.
Arguments:
- pairs: bfloat16 [64, 1024, 1024], P(None, 'row', 'col'), may hold values from -6 to 6
- weights_first: bfloat16 [3, 3, 64, 64], replicated, may hold values from -0.25 to 0.25
- weights_second: bfloat16 [3, 3, 64, 64], replicated, may hold values from -0.25 to 0.25
- gains: float32 [2, 64], replicated, may hold values from 0.5 to 1.5
- shifts: float32 [2, 64], replicated, may hold values from -3 to 3
- dilations: int32 [2], replicated, may hold values from 1 to 16, as said below
- residue_count: int32 [1], replicated, may hold values from 768 to 1024
- cotangent: bfloat16 [64, 1024, 1024], P(None, 'row', 'col'), may hold values from -6 to 6
Outputs:
- symmetric: bfloat16 [64, 1024, 1024], P(None, 'row', 'col')
- grad_pairs: bfloat16 [64, 1024, 1024], P(None, 'row', 'col')
- grad_weights: float32 [2, 3, 3, 64, 64], replicated
Inputs may be any that keep to these rules, and one draw needn't show every extreme that they name: `dilations`: each is a power of two; one of the two equals 16, the other is smaller.
All inputs are finite; a program needn't handle non-finite values.
Results may differ from a plain program's by a relative error of at most 0.0054.
Values may be sent and summed in bfloat16 or wider, within the bound.
A program may use at most 128 MiB of HBM per device.

v0:
```python
import jax
import jax.numpy as jnp
from jax import lax
from jax.sharding import PartitionSpec as P

MAX_DILATION = 16


EPSILON = 1e-05


def with_halo(block, sides, width):
    for axis, dim in sides:
        count = lax.axis_size(axis)
        forward = [(i, i + 1) for i in range(count - 1)]
        backward = [(target, source) for source, target in forward]
        low = lax.ppermute(
            lax.slice_in_dim(block, block.shape[dim] - width, None, axis=dim), axis, forward
        )
        high = lax.ppermute(lax.slice_in_dim(block, 0, width, axis=dim), axis, backward)
        block = jnp.concatenate([low, block, high], axis=dim)
    return block


def widen(field):
    return with_halo(field, (("row", 1), ("col", 2)), MAX_DILATION)


def channel_sums(values):
    return lax.psum(values, ("row", "col"))


def mirror(stacked, row_count, col_count):
    layers, chans, rows, cols = stacked.shape
    split = rows // col_count
    factor = row_count // col_count
    arranged = stacked.reshape(layers, chans, col_count, split, factor, rows)
    arranged = arranged.transpose(0, 1, 2, 4, 3, 5).reshape(
        layers, chans, col_count, factor, split * rows
    )
    arranged = lax.all_to_all(arranged, "col", split_axis=2, concat_axis=3, tiled=True)
    arranged = lax.all_to_all(
        lax.all_to_all(arranged, "row", split_axis=3, concat_axis=3, tiled=True),
        "col",
        split_axis=3,
        concat_axis=2,
        tiled=True,
    )
    arranged = arranged.reshape(layers, chans, col_count, factor, split, rows)
    return arranged.transpose(0, 1, 5, 3, 2, 4).reshape(layers, chans, rows, cols)


def window(padded, down, right, rows, cols):
    start_row = MAX_DILATION + down
    start_col = MAX_DILATION + right
    return lax.dynamic_slice(
        padded, (jnp.int32(0), start_row, start_col), (padded.shape[0], rows, cols)
    )


def convolve(padded, weights, dilation, rows, cols):
    chans = padded.shape[0]
    summed = jnp.zeros((weights.shape[2], rows * cols), jnp.float32)
    for vertical in range(3):
        for lateral in range(3):
            portion = window(
                padded, (vertical - 1) * dilation, (lateral - 1) * dilation, rows, cols
            )
            summed = summed + jnp.dot(
                weights[vertical, lateral],
                portion.reshape(chans, rows * cols),
                preferred_element_type=jnp.float32,
            )
    return summed.reshape(weights.shape[2], rows, cols)


def convolve_back(padded, weights, dilation, rows, cols):
    chans = padded.shape[0]
    summed = jnp.zeros((weights.shape[3], rows * cols), jnp.float32)
    for vertical in range(3):
        for lateral in range(3):
            portion = window(
                padded, (1 - vertical) * dilation, (1 - lateral) * dilation, rows, cols
            )
            summed = summed + jnp.dot(
                weights[vertical, lateral].T,
                portion.reshape(chans, rows * cols),
                preferred_element_type=jnp.float32,
            )
    return summed.reshape(weights.shape[3], rows, cols)


def weight_grad(grad, padded, dilation, rows, cols):
    chans = padded.shape[0]
    flat = grad.reshape(grad.shape[0], rows * cols)
    blocks = []
    for vertical in range(3):
        across = []
        for lateral in range(3):
            portion = window(
                padded, (vertical - 1) * dilation, (lateral - 1) * dilation, rows, cols
            )
            across.append(
                lax.dot_general(
                    flat,
                    portion.reshape(chans, rows * cols),
                    (((1,), (1,)), ((), ())),
                    preferred_element_type=jnp.float32,
                )
            )
        blocks.append(jnp.stack(across))
    return jnp.stack(blocks)


def normalize(hidden, valid, count, gain, shift):
    center = channel_sums((jnp.sum(hidden * valid, axis=(1, 2)),))[0] / count
    centered = hidden - center[:, None, None]
    spread = channel_sums((jnp.sum(centered * centered * valid, axis=(1, 2)),))[0] / count
    inverse = lax.rsqrt(spread + EPSILON)
    normed = centered * inverse[:, None, None]
    return (normed, inverse, normed * gain[:, None, None] + shift[:, None, None])


def norm_back(upstream, normed, inverse, valid, count, gain):
    scaled = upstream * gain[:, None, None]
    totals = channel_sums(
        (jnp.sum(scaled * valid, axis=(1, 2)), jnp.sum(scaled * normed * valid, axis=(1, 2)))
    )
    first = totals[0] / count
    second = totals[1] / count
    return (
        valid
        * inverse[:, None, None]
        * (scaled - first[:, None, None] - normed * second[:, None, None])
    ).astype(jnp.bfloat16)


def per_device(
    pairs, weights_first, weights_second, gains, shifts, dilations, residue_count, cotangent
):
    chans, rows, cols = pairs.shape
    row_count = lax.axis_size("row")
    col_count = lax.axis_size("col")
    row_place = lax.axis_index("row") * rows + jnp.arange(rows, dtype=jnp.int32)
    col_place = lax.axis_index("col") * cols + jnp.arange(cols, dtype=jnp.int32)
    row_marker = (row_place < residue_count[0]).astype(jnp.float32)
    col_marker = (col_place < residue_count[0]).astype(jnp.float32)
    valid = row_marker[:, None] * col_marker[None, :]
    count = residue_count[0].astype(jnp.float32) ** 2
    masked = pairs * valid.astype(jnp.bfloat16)
    masked_pad = widen(masked)
    first = convolve(masked_pad, weights_first, dilations[0], rows, cols)
    normed_one, inverse_one, level_one = normalize(first, valid, count, gains[0], shifts[0])
    active = (valid * jax.nn.elu(level_one)).astype(jnp.bfloat16)
    active_pad = widen(active)
    second = convolve(active_pad, weights_second, dilations[1], rows, cols)
    normed_two, inverse_two, level_two = normalize(second, valid, count, gains[1], shifts[1])
    before = masked.astype(jnp.float32) + level_two
    final = (valid * jax.nn.elu(before)).astype(jnp.bfloat16)
    cot_flip = mirror(cotangent[None], row_count, col_count)[0]
    final_flip = mirror(final[None], row_count, col_count)[0]
    symmetric = ((final.astype(jnp.float32) + final_flip.astype(jnp.float32)) * 0.5).astype(
        jnp.bfloat16
    )
    back = (cotangent.astype(jnp.float32) + cot_flip.astype(jnp.float32)) * 0.5
    outer = back * valid * jnp.exp(jnp.minimum(before, 0.0))
    grad_two = norm_back(outer, normed_two, inverse_two, valid, count, gains[1])
    upward = convolve_back(widen(grad_two), weights_second, dilations[1], rows, cols)
    inner = upward * valid * jnp.exp(jnp.minimum(level_one, 0.0))
    grad_one = norm_back(inner, normed_one, inverse_one, valid, count, gains[0])
    lower = convolve_back(widen(grad_one), weights_first, dilations[0], rows, cols)
    grad_pairs = (valid * (outer + lower)).astype(jnp.bfloat16)
    partial_one = weight_grad(grad_one, masked_pad, dilations[0], rows, cols)
    partial_two = weight_grad(grad_two, active_pad, dilations[1], rows, cols)
    total_one, total_two = channel_sums((partial_one, partial_two))
    return (symmetric, grad_pairs, jnp.stack([total_one, total_two]))


def solution(mesh):
    in_specs = (P(None, "row", "col"), P(), P(), P(), P(), P(), P(), P(None, "row", "col"))
    out_specs = (P(None, "row", "col"), P(None, "row", "col"), P())
    return jax.shard_map(
        per_device, mesh=mesh, in_specs=in_specs, out_specs=out_specs, check_vma=False
    )
```

profile of v0, /device:TPU:1, one launch (start us, length us, event | category | flops | bytes accessed | tf_op | source)
XLA Modules:
  0.0 1051.5 jit_solution(5737878448196673734)
XLA Ops:
  9.2 9.7 collective-permute-start
  24.9 11.3 %collective-permute-done.1 = bf16[64,16,128]{2,0,1:T(8,128)(2,1)S(1)} collective-permute-done((bf16[64,16,128]{2,0,1:T(8,128)(2,1)S(1)}, bf16[64,16,128]{2,0,1:T(8,128)(2,1)S(1)}, u32[]{:S(2)}, u32[]{:S(2)}) %collective-permute-start.1) | collective-permute-done | bytes 262176 | tf_op jit(solution)/shard_map/ppermute | solution.py:20
  43.7 7.8 collective-permute-start.2
  68.1 78.2 %psum.70 = f32[64]{0:T(128)S(1)} all-reduce(f32[64]{0:T(128)S(1)} %get-tuple-element.82), channel_id=1, replica_groups=mesh['row'=32,'col'=8] {'row','col'}, use_global_device_ids=true, to_apply=%region_1.0 | all-reduce | flops 64 | bytes 512 | tf_op jit(solution)/shard_map/psum | solution.py:30
  146.6 73.1 %psum.71 = f32[64]{0:T(128)S(1)} all-reduce(f32[64]{0:T(128)S(1)} %multiply_reduce_fusion.4), channel_id=1, replica_groups=mesh['row'=32,'col'=8] {'row','col'}, use_global_device_ids=true, to_apply=%region_3.0 | all-reduce | flops 64 | bytes 512 | tf_op jit(solution)/shard_map/psum | solution.py:30
  220.4 5.0 collective-permute-start.4
  226.7 12.0 %collective-permute-done.4 = bf16[64,16,128]{2,0,1:T(8,128)(2,1)S(1)} collective-permute-done((bf16[64,16,128]{2,0,1:T(8,128)(2,1)S(1)}, bf16[64,16,128]{2,0,1:T(8,128)(2,1)S(1)}, u32[]{:S(2)}, u32[]{:S(2)}) %collective-permute-start.4) | collective-permute-done | bytes 262176 | tf_op jit(solution)/shard_map/ppermute | solution.py:17
  238.7 7.2 collective-permute-done.5
  251.4 9.3 collective-permute-start.6
  272.9 4.1 all-to-all-start.3
  294.3 9.5 all-to-all-start.4
  307.7 13.4 %all-to-all-done.4 = bf16[1,64,1,32,128]{4,1,2,0,3:T(8,128)(2,1)} async-done(((bf16[1,64,1,32,128]{4,1,2,0,3:T(8,128)(2,1)}), bf16[1,64,1,32,128]{4,1,2,0,3:T(8,128)(2,1)}, u32[]{:S(2)}, u32[]{:S(2)}) %all-to-all-start.4) | async-done | bytes 524320 | tf_op jit(solution)/shard_map/all_to_all | solution.py:43
  321.1 8.5 all-to-all-start.5
  331.4 74.1 %psum.72 = f32[64]{0:T(128)S(1)} all-reduce(f32[64]{0:T(128)S(1)} %get-tuple-element.84), channel_id=1, replica_groups=mesh['row'=32,'col'=8] {'row','col'}, use_global_device_ids=true, to_apply=%region_5.6 | all-reduce | flops 64 | bytes 512 | tf_op jit(solution)/shard_map/psum | solution.py:30
  405.8 72.7 %psum.73 = f32[64]{0:T(128)S(1)} all-reduce(f32[64]{0:T(128)S(1)} %fusion.24), channel_id=1, replica_groups=mesh['row'=32,'col'=8] {'row','col'}, use_global_device_ids=true, to_apply=%region_7.8 | all-reduce | flops 64 | bytes 512 | tf_op jit(solution)/shard_map/psum | solution.py:30
  487.6 4.0 multiply_reduce_fusion.3
  491.7 74.1 %all-reduce.1 = (f32[64]{0:T(128)S(1)}, f32[64]{0:T(128)S(1)}) all-reduce(f32[64]{0:T(128)S(1)} %get-tuple-element.13, f32[64]{0:T(128)S(1)} %get-tuple-element.12), channel_id=1, replica_groups=mesh['row'=32,'col'=8] {'row','col'}, use_global_device_ids=true, to_apply=%region_11.12 | all-reduce | flops 128 | bytes 1024 | tf_op jit(solution)/shard_map/psum | solution.py:30
  572.1 5.2 collective-permute-start.8
  579.8 11.1 %collective-permute-done.8 = bf16[64,16,128]{2,0,1:T(8,128)(2,1)S(1)} collective-permute-done((bf16[64,16,128]{2,0,1:T(8,128)(2,1)S(1)}, bf16[64,16,128]{2,0,1:T(8,128)(2,1)S(1)}, u32[]{:S(2)}, u32[]{:S(2)}) %collective-permute-start.8) | collective-permute-done | bytes 262176 | tf_op jit(solution)/shard_map/ppermute | solution.py:17
  590.9 6.3 collective-permute-done.9
  608.0 8.2 collective-permute-start.10
  636.8 75.1 %all-reduce = (f32[64]{0:T(128)S(1)}, f32[64]{0:T(128)S(1)}) all-reduce(f32[64]{0:T(128)S(1)} %get-tuple-element.15, f32[64]{0:T(128)S(1)} %get-tuple-element.14), channel_id=1, replica_groups=mesh['row'=32,'col'=8] {'row','col'}, use_global_device_ids=true, to_apply=%region_15.16 | all-reduce | flops 128 | bytes 1024 | tf_op jit(solution)/shard_map/psum | solution.py:30
  717.6 4.9 collective-permute-start.12
  724.6 11.3 %collective-permute-done.12 = bf16[64,16,128]{2,0,1:T(8,128)(2,1)S(1)} collective-permute-done((bf16[64,16,128]{2,0,1:T(8,128)(2,1)S(1)}, bf16[64,16,128]{2,0,1:T(8,128)(2,1)S(1)}, u32[]{:S(2)}, u32[]{:S(2)}) %collective-permute-start.12) | collective-permute-done | bytes 262176 | tf_op jit(solution)/shard_map/ppermute | solution.py:17
  735.9 5.8 collective-permute-done.13
  744.8 11.0 %collective-permute-start.14 = (bf16[64,64,16]{1,2,0:T(8,128)(2,1)}, bf16[64,64,16]{1,2,0:T(8,128)(2,1)}, u32[]{:S(2)}, u32[]{:S(2)}) collective-permute-start(bf16[64,64,16]{1,2,0:T(8,128)(2,1)} %copy.126), channel_id=1, source_target_pairs={{0,1},{1,2},{2,3},{3,4},{4,5},{5,6},{6,7},{8,9},{9,10},{10,11},{11... | collective-permute-start | bytes 393224 | tf_op jit(solution)/shard_map/ppermute | solution.py:17
  761.3 4.4 all-to-all-start
  765.6 211.0 %all-reduce.5.cloned.1.call-done = (f32[1,3,3,64,64]{4,3,2,1,0:T(8,128)}, f32[1,3,3,64,64]{4,3,2,1,0:T(8,128)}) async-done(((f32[1,3,3,64,64]{4,3,2,1,0:T(8,128)}, f32[1,3,3,64,64]{4,3,2,1,0:T(8,128)}), (f32[1,3,3,64,64]{4,3,2,1,0:T(8,128)}, f32[1,3,3,64,64]{4,3,2,1,0:T(8,128)})) %all-reduce.5.cloned.1.call-update) | async-done | bytes 294928 | tf_op jit(solution)/shard_map/psum | solution.py:30
  990.1 7.6 all-to-all-start.1
  1002.1 9.4 all-to-all-done.1
  1011.4 11.3 %all-to-all-start.2 = ((bf16[1,64,1,32,128]{4,1,2,0,3:T(8,128)(2,1)}), bf16[1,64,1,32,128]{4,1,2,0,3:T(8,128)(2,1)}, u32[]{:S(2)}, u32[]{:S(2)}) async-start(bf16[1,64,1,32,128]{4,1,2,0,3:T(8,128)(2,1)} %all-to-all-done.1), calls=%async_computation.2 | async-start | bytes 1048576 | tf_op jit(solution)/shard_map/all_to_all | solution.py:42
  1027.3 10.0 all-to-all-done.2
  (211 shorter events, 163.9 us)
Async XLA Ops:
  7.2 13.0 %copy-start.23 = (s32[2]{0:T(128)S(1)}, s32[2]{0:T(128)}, u32[]{:S(2)}) copy-start(s32[2]{0:T(128)} %param.13) | copy-start | bytes 28
  9.2 51.0 %copy-start.6 = (bf16[64,32,128]{2,0,1:T(8,128)(2,1)}, bf16[64,32,128]{2,0,1:T(8,128)(2,1)S(1)}, u32[]{:S(2)}) copy-start(bf16[64,32,128]{2,0,1:T(8,128)(2,1)S(1)} %copy_multiply_fusion) | copy-start | bytes 1572868
  9.2 15.7 %collective-permute-start = (bf16[64,16,128]{2,0,1:T(8,128)(2,1)S(1)}, bf16[64,16,128]{2,0,1:T(8,128)(2,1)S(1)}, u32[]{:S(2)}, u32[]{:S(2)}) collective-permute-start(bf16[64,16,128]{2,0,1:T(8,128)(2,1)S(1)} %get-tuple-element.71), channel_id=1, source_target_pairs={{0,8},{8,16},{16,24},{24,32},{32,40},{40,48},{48,56},{56,64},{64,7... | collective-permute-start | bytes 786440 | tf_op jit(solution)/shard_map/ppermute | solution.py:17
  18.9 17.3 %collective-permute-start.1 = (bf16[64,16,128]{2,0,1:T(8,128)(2,1)S(1)}, bf16[64,16,128]{2,0,1:T(8,128)(2,1)S(1)}, u32[]{:S(2)}, u32[]{:S(2)}) collective-permute-start(bf16[64,16,128]{2,0,1:T(8,128)(2,1)S(1)} %get-tuple-element.72), channel_id=1, source_target_pairs={{8,0},{16,8},{24,16},{32,24},{40,32},{48,40},{56,48},{64,56},{72,6... | collective-permute-start | bytes 786440 | tf_op jit(solution)/shard_map/ppermute | solution.py:20
  36.8 14.7 %copy-start.25 = (f32[2,64]{1,0:T(2,128)S(1)}, f32[2,64]{1,0:T(2,128)}, u32[]{:S(2)}) copy-start(f32[2,64]{1,0:T(2,128)} %param.12) | copy-start | bytes 1540
  39.8 17.9 %collective-permute-start.3 = (bf16[64,64,16]{1,2,0:T(8,128)(2,1)S(1)}, bf16[64,64,16]{1,2,0:T(8,128)(2,1)S(1)}, u32[]{:S(2)}, u32[]{:S(2)}) collective-permute-start(bf16[64,64,16]{1,2,0:T(8,128)(2,1)S(1)} %copy.71), channel_id=1, source_target_pairs={{1,0},{2,1},{3,2},{4,3},{5,4},{6,5},{7,6},{9,8},{10,9},{11,10},{12... | collective-permute-start | bytes 393224 | tf_op jit(solution)/shard_map/ppermute | solution.py:20
  43.7 11.4 %collective-permute-start.2 = (bf16[64,64,16]{1,2,0:T(8,128)(2,1)}, bf16[64,64,16]{1,2,0:T(8,128)(2,1)S(1)}, u32[]{:S(2)}, u32[]{:S(2)}) collective-permute-start(bf16[64,64,16]{1,2,0:T(8,128)(2,1)} %copy.70), channel_id=1, source_target_pairs={{0,1},{1,2},{2,3},{3,4},{4,5},{5,6},{6,7},{8,9},{9,10},{10,11},{11... | collective-permute-start | bytes 393224 | tf_op jit(solution)/shard_map/ppermute | solution.py:17
  68.1 237.3 %copy-start.2 = (f32[4096,64]{0,1:T(8,128)}, f32[4096,64]{0,1:T(8,128)S(1)}, u32[]{:S(2)}) copy-start(f32[4096,64]{0,1:T(8,128)S(1)} %get-tuple-element.83) | copy-start | bytes 3145732
  220.4 25.5 %copy-start.8 = (bf16[64,32,128]{2,0,1:T(8,128)(2,1)}, bf16[64,32,128]{2,0,1:T(8,128)(2,1)S(1)}, u32[]{:S(2)}) copy-start(bf16[64,32,128]{2,0,1:T(8,128)(2,1)S(1)} %fusion.3) | copy-start | bytes 1572868
  220.4 18.2 %collective-permute-start.4 = (bf16[64,16,128]{2,0,1:T(8,128)(2,1)S(1)}, bf16[64,16,128]{2,0,1:T(8,128)(2,1)S(1)}, u32[]{:S(2)}, u32[]{:S(2)}) collective-permute-start(bf16[64,16,128]{2,0,1:T(8,128)(2,1)S(1)} %get-tuple-element.69), channel_id=1, source_target_pairs={{0,8},{8,16},{16,24},{24,32},{32,40},{40,48},{48,56},{56,64},{64,7... | collective-permute-start | bytes 786440 | tf_op jit(solution)/shard_map/ppermute | solution.py:17
  225.4 20.4 %collective-permute-start.5 = (bf16[64,16,128]{2,0,1:T(8,128)(2,1)S(1)}, bf16[64,16,128]{2,0,1:T(8,128)(2,1)S(1)}, u32[]{:S(2)}, u32[]{:S(2)}) collective-permute-start(bf16[64,16,128]{2,0,1:T(8,128)(2,1)S(1)} %get-tuple-element.70), channel_id=1, source_target_pairs={{8,0},{16,8},{24,16},{32,24},{40,32},{48,40},{56,48},{64,56},{72,6... | collective-permute-start | bytes 786440 | tf_op jit(solution)/shard_map/ppermute | solution.py:20
  251.4 28.0 %collective-permute-start.6 = (bf16[64,64,16]{1,2,0:T(8,128)(2,1)}, bf16[64,64,16]{1,2,0:T(8,128)(2,1)}, u32[]{:S(2)}, u32[]{:S(2)}) collective-permute-start(bf16[64,64,16]{1,2,0:T(8,128)(2,1)} %copy.84), channel_id=1, source_target_pairs={{0,1},{1,2},{2,3},{3,4},{4,5},{5,6},{6,7},{8,9},{9,10},{10,11},{11... | collective-permute-start | bytes 393224 | tf_op jit(solution)/shard_map/ppermute | solution.py:17
  263.7 19.2 %collective-permute-start.7 = (bf16[64,64,16]{1,2,0:T(8,128)(2,1)}, bf16[64,64,16]{1,2,0:T(8,128)(2,1)}, u32[]{:S(2)}, u32[]{:S(2)}) collective-permute-start(bf16[64,64,16]{1,2,0:T(8,128)(2,1)} %copy.85), channel_id=1, source_target_pairs={{1,0},{2,1},{3,2},{4,3},{5,4},{6,5},{7,6},{9,8},{10,9},{11,10},{12... | collective-permute-start | bytes 393224 | tf_op jit(solution)/shard_map/ppermute | solution.py:20
  272.9 21.4 %all-to-all-start.3 = ((bf16[1,64,8,4,128]{4,1,3,0,2:T(8,128)(2,1)}), bf16[1,64,8,4,128]{4,1,3,0,2:T(8,128)(2,1)}, u32[]{:S(2)}, u32[]{:S(2)}) async-start(bf16[1,64,8,4,128]{4,1,3,0,2:T(8,128)(2,1)} %copy.107), calls=%async_computation.3 | async-start | bytes 1048576 | tf_op jit(solution)/shard_map/all_to_all | solution.py:41
  294.3 26.8 %all-to-all-start.4 = ((bf16[1,64,1,32,128]{4,1,2,0,3:T(8,128)(2,1)}), bf16[1,64,1,32,128]{4,1,2,0,3:T(8,128)(2,1)}, u32[]{:S(2)}, u32[]{:S(2)}) async-start(bf16[1,64,1,32,128]{4,1,2,0,3:T(8,128)(2,1)} %bitcast.51), calls=%async_computation.4 | async-start | bytes 1048576 | tf_op jit(solution)/shard_map/all_to_all | solution.py:43
  321.1 157.4 %all-to-all-start.5 = ((bf16[1,64,1,32,128]{4,1,2,0,3:T(8,128)(2,1)}), bf16[1,64,1,32,128]{4,1,2,0,3:T(8,128)(2,1)}, u32[]{:S(2)}, u32[]{:S(2)}) async-start(bf16[1,64,1,32,128]{4,1,2,0,3:T(8,128)(2,1)} %all-to-all-done.4), calls=%async_computation.5 | async-start | bytes 1048576 | tf_op jit(solution)/shard_map/all_to_all | solution.py:42
  329.6 647.0 %all-reduce.5.cloned.1.call-start = ((), (), s32[]{:S(2)}) async-start(), calls=%async_computation.6 | async-start | bytes 1179648 | tf_op jit(solution)/shard_map/psum | solution.py:30
  331.4 156.2 %copy-start.5 = (f32[4096,64]{0,1:T(8,128)}, f32[4096,64]{0,1:T(8,128)S(1)}, u32[]{:S(2)}) copy-start(f32[4096,64]{0,1:T(8,128)S(1)} %get-tuple-element.85) | copy-start | bytes 3145732
  491.6 76.2 %copy-start.9 = (bf16[64,32,128]{2,0,1:T(8,128)(2,1)S(1)}, bf16[64,32,128]{2,0,1:T(8,128)(2,1)}, u32[]{:S(2)}) copy-start(bf16[64,32,128]{2,0,1:T(8,128)(2,1)} %copy-done.8) | copy-start | bytes 1572868
  572.1 18.8 %collective-permute-start.8 = (bf16[64,16,128]{2,0,1:T(8,128)(2,1)S(1)}, bf16[64,16,128]{2,0,1:T(8,128)(2,1)S(1)}, u32[]{:S(2)}, u32[]{:S(2)}) collective-permute-start(bf16[64,16,128]{2,0,1:T(8,128)(2,1)S(1)} %get-tuple-element.67), channel_id=1, source_target_pairs={{0,8},{8,16},{16,24},{24,32},{32,40},{40,48},{48,56},{56,64},{64,7... | collective-permute-start | bytes 786440 | tf_op jit(solution)/shard_map/ppermute | solution.py:17
  577.3 19.9 %collective-permute-start.9 = (bf16[64,16,128]{2,0,1:T(8,128)(2,1)S(1)}, bf16[64,16,128]{2,0,1:T(8,128)(2,1)S(1)}, u32[]{:S(2)}, u32[]{:S(2)}) collective-permute-start(bf16[64,16,128]{2,0,1:T(8,128)(2,1)S(1)} %get-tuple-element.68), channel_id=1, source_target_pairs={{8,0},{16,8},{24,16},{32,24},{40,32},{48,40},{56,48},{64,56},{72,6... | collective-permute-start | bytes 786440 | tf_op jit(solution)/shard_map/ppermute | solution.py:20
  605.0 18.2 %collective-permute-start.11 = (bf16[64,64,16]{1,2,0:T(8,128)(2,1)}, bf16[64,64,16]{1,2,0:T(8,128)(2,1)}, u32[]{:S(2)}, u32[]{:S(2)}) collective-permute-start(bf16[64,64,16]{1,2,0:T(8,128)(2,1)} %copy.113), channel_id=1, source_target_pairs={{1,0},{2,1},{3,2},{4,3},{5,4},{6,5},{7,6},{9,8},{10,9},{11,10},{12... | collective-permute-start | bytes 393224 | tf_op jit(solution)/shard_map/ppermute | solution.py:20
  608.0 11.8 %collective-permute-start.10 = (bf16[64,64,16]{1,2,0:T(8,128)(2,1)}, bf16[64,64,16]{1,2,0:T(8,128)(2,1)}, u32[]{:S(2)}, u32[]{:S(2)}) collective-permute-start(bf16[64,64,16]{1,2,0:T(8,128)(2,1)} %copy.112), channel_id=1, source_target_pairs={{0,1},{1,2},{2,3},{3,4},{4,5},{5,6},{6,7},{8,9},{9,10},{10,11},{11... | collective-permute-start | bytes 393224 | tf_op jit(solution)/shard_map/ppermute | solution.py:17
  636.8 77.3 %copy-start.7 = (bf16[64,32,128]{2,0,1:T(8,128)(2,1)S(1)}, bf16[64,32,128]{2,0,1:T(8,128)(2,1)}, u32[]{:S(2)}) copy-start(bf16[64,32,128]{2,0,1:T(8,128)(2,1)} %copy-done.6) | copy-start | bytes 1572868
  717.6 18.3 %collective-permute-start.12 = (bf16[64,16,128]{2,0,1:T(8,128)(2,1)S(1)}, bf16[64,16,128]{2,0,1:T(8,128)(2,1)S(1)}, u32[]{:S(2)}, u32[]{:S(2)}) collective-permute-start(bf16[64,16,128]{2,0,1:T(8,128)(2,1)S(1)} %get-tuple-element.65), channel_id=1, source_target_pairs={{0,8},{8,16},{16,24},{24,32},{32,40},{40,48},{48,56},{56,64},{64,7... | collective-permute-start | bytes 786440 | tf_op jit(solution)/shard_map/ppermute | solution.py:17
  722.5 19.2 %collective-permute-start.13 = (bf16[64,16,128]{2,0,1:T(8,128)(2,1)S(1)}, bf16[64,16,128]{2,0,1:T(8,128)(2,1)S(1)}, u32[]{:S(2)}, u32[]{:S(2)}) collective-permute-start(bf16[64,16,128]{2,0,1:T(8,128)(2,1)S(1)} %get-tuple-element.66), channel_id=1, source_target_pairs={{8,0},{16,8},{24,16},{32,24},{40,32},{48,40},{56,48},{64,56},{72,6... | collective-permute-start | bytes 786440 | tf_op jit(solution)/shard_map/ppermute | solution.py:20
  742.9 16.6 %copy-start.12 = (bf16[64,32,128]{2,0,1:T(8,128)(2,1)S(1)}, bf16[64,32,128]{2,0,1:T(8,128)(2,1)}, u32[]{:S(2)}) copy-start(bf16[64,32,128]{2,0,1:T(8,128)(2,1)} %get-tuple-element.56) | copy-start | bytes 1572868
  744.8 233.8 %collective-permute-start.14 = (bf16[64,64,16]{1,2,0:T(8,128)(2,1)}, bf16[64,64,16]{1,2,0:T(8,128)(2,1)}, u32[]{:S(2)}, u32[]{:S(2)}) collective-permute-start(bf16[64,64,16]{1,2,0:T(8,128)(2,1)} %copy.126), channel_id=1, source_target_pairs={{0,1},{1,2},{2,3},{3,4},{4,5},{5,6},{6,7},{8,9},{9,10},{10,11},{11... | collective-permute-start | bytes 393224 | tf_op jit(solution)/shard_map/ppermute | solution.py:17
  757.6 223.5 %collective-permute-start.15 = (bf16[64,64,16]{1,2,0:T(8,128)(2,1)}, bf16[64,64,16]{1,2,0:T(8,128)(2,1)}, u32[]{:S(2)}, u32[]{:S(2)}) collective-permute-start(bf16[64,64,16]{1,2,0:T(8,128)(2,1)} %copy.127), channel_id=1, source_target_pairs={{1,0},{2,1},{3,2},{4,3},{5,4},{6,5},{7,6},{9,8},{10,9},{11,10},{12... | collective-permute-start | bytes 393224 | tf_op jit(solution)/shard_map/ppermute | solution.py:20
  761.3 228.8 %all-to-all-start = ((bf16[1,64,8,4,128]{4,1,3,0,2:T(8,128)(2,1)}), bf16[1,64,8,4,128]{4,1,3,0,2:T(8,128)(2,1)}, u32[]{:S(2)}, u32[]{:S(2)}) async-start(bf16[1,64,8,4,128]{4,1,3,0,2:T(8,128)(2,1)} %copy.99), calls=%async_computation | async-start | bytes 1048576 | tf_op jit(solution)/shard_map/all_to_all | solution.py:41
  990.1 21.3 %all-to-all-start.1 = ((bf16[1,64,1,32,128]{4,1,2,0,3:T(8,128)(2,1)}), bf16[1,64,1,32,128]{4,1,2,0,3:T(8,128)(2,1)}, u32[]{:S(2)}, u32[]{:S(2)}) async-start(bf16[1,64,1,32,128]{4,1,2,0,3:T(8,128)(2,1)} %bitcast.43), calls=%async_computation.1 | async-start | bytes 1048576 | tf_op jit(solution)/shard_map/all_to_all | solution.py:43
  1011.4 25.9 %all-to-all-start.2 = ((bf16[1,64,1,32,128]{4,1,2,0,3:T(8,128)(2,1)}), bf16[1,64,1,32,128]{4,1,2,0,3:T(8,128)(2,1)}, u32[]{:S(2)}, u32[]{:S(2)}) async-start(bf16[1,64,1,32,128]{4,1,2,0,3:T(8,128)(2,1)} %all-to-all-done.1), calls=%async_computation.2 | async-start | bytes 1048576 | tf_op jit(solution)/shard_map/all_to_all | solution.py:42
  (17 other events, 41.9 us)
Sparse Core Ops, SparseCore 0:
  724.8 251.8 all-reduce.4
where the time goes:
time: 1060 us; the launch traced here: 1050 us
  blocking collectives  447 us (42%)
  waiting for transfers between devices  316 us (30%)
  starting transfers between devices  122 us (12%)
  local copies, waits for them, and re-layouts  83.1 us (8%)
  other arithmetic  31.3 us (3%)
  matrix products  30.3 us (3%)
  between operations  21.4 us (2%)
    psum x6, blocking collectives, channel_sums(): return lax.psum(values, ('row', 'col'))  447 us
    psum x1, waiting for transfers between devices, channel_sums(): return lax.psum(values, ('row', 'col'))  211 us
    ppermute x8, starting transfers between devices, with_halo(): lax.ppermute(lax.slice_in_dim(block, block.shape[dim] - width, None, axis...  60.9 us
    ppermute x8, waiting for transfers between devices, with_halo(): lax.ppermute(lax.slice_in_dim(block, block.shape[dim] - width, None, axis...  41.3 us
    ppermute x8, waiting for transfers between devices, with_halo(): lax.ppermute(lax.slice_in_dim(block, 0, width, axis=dim), axis, backward)  30.6 us
    all_to_all x2, waiting for transfers between devices, mirror(): lax.all_to_all(arranged, 'row', split_axis=3, concat_axis=3, tiled=True)  22.8 us
  transfers between devices with their start and end apart: 23, of which 14 were waited for; matrix products, arithmetic and copies ran while one was open for 6% of the time, Pallas kernels for 0%

commit v1 on v0

v1 whole, which is shorter than its diff:
```python
import functools

import jax
import jax.numpy as jnp
from jax import lax
from jax.experimental import pallas as pl
from jax.experimental.pallas import tpu as pltpu
from jax.sharding import PartitionSpec as P

MESH = pl.DeviceIdType.MESH
F32 = jnp.float32
BF16 = jnp.bfloat16
EPSILON = 1e-05
EDGE = 16
PAIRS, ACTIVE, GRAD_TWO, GRAD_ONE = range(4)


def roll(x, shift):
    return pltpu.roll(x, shift, 1)


def kernel(
    R,
    C,
    dil_ref,
    count_ref,
    pairs_ref,
    cot_ref,
    w_first_ref,
    w_second_ref,
    gains_ref,
    shifts_ref,
    sym_ref,
    gp_ref,
    gw_ref,
    pin,
    cin,
    fin_out,
    fin_in,
    gp_out,
    mir_s,
    mir_r,
    ext,
    lat_s,
    lat_r,
    taps,
    S,
    Sb,
    first,
    second,
    slope_one,
    outer,
    inner,
    wmat,
    gain_b,
    shift_b,
    ar_s,
    ar_r,
    w_acc,
    w_parts,
    w_a,
    w_b_s,
    w_b,
    w_c_s,
    w_c,
    tile_send,
    tile_recv,
    halo_send,
    halo_recv,
    mir_send,
    mir_recv,
    ar_send_sem,
    ar_recv_sem,
    w_send_sem,
    w_recv_sem,
):
    CH, RT, CT = 64, 32, 128
    row = lax.axis_index("row")
    col = lax.axis_index("col")
    half = C // 2
    G1, G2 = 2 * C, R // 2
    share = 16 // G1
    m, p = row // 2, (row % 2) * C + col

    def place(tr, tc):
        z = (C - tc) % C
        return 2 * (tr // 2) + z // half, 2 * (z % half) + tr % 2

    def tile_of(r, c):
        z = (r % 2) * half + c // 2
        return 2 * (r // 2) + c % 2, (C - z) % C

    def holder(tr, tc):
        return tr, tc

    lr, lc = tile_of(row, col)
    up, down = (lr + R - 1) % R, (lr + 1) % R
    left, right = (lc + C - 1) % C, (lc + 1) % C

    def is_me(target):
        return jnp.logical_and(target[0] == row, target[1] == col)

    def remote(src, dst, send, recv, target):
        return pltpu.make_async_remote_copy(
            src_ref=src,
            dst_ref=dst,
            send_sem=send,
            recv_sem=recv,
            device_id=target,
            device_id_type=MESH,
        )

    def wait_bytes(ref, sem):
        pltpu.make_async_copy(ref, ref, sem).wait()

    barrier = pltpu.get_barrier_semaphore()

    def greet(target):
        pl.semaphore_signal(barrier, inc=1, device_id=target, device_id_type=MESH)

    def greet_one(k, _):
        t = (p + k) % G1
        greet((2 * m + t // C, t % C))
        return 0

    def greet_two(k, _):
        t = (m + k) % G2
        greet((2 * t + row % 2, col))
        return 0

    lax.fori_loop(1, G1, greet_one, 0)
    lax.fori_loop(1, G2, greet_two, 0)
    across = (lr + R - 1 + 2 * (lr % 2)) % R
    for tc in (left, lc, right):
        greet(place(across, tc))
    expected = G1 - 1 + G2 - 1 + 3
    for b in range(4):
        for target in (place(4 * col + b, row // 4), holder(4 * lc + b, lr // 4)):
            other = jnp.logical_not(is_me(target))
            expected = expected + other.astype(jnp.int32)

            @pl.when(other)
            def _(target=target):
                greet(target)

    n = count_ref[0]
    count = jnp.full((1, CT), 1.0, F32) * (n.astype(F32) * n.astype(F32))
    lane = lax.broadcasted_iota(jnp.int32, (CH, CT), 1)
    lane_row = lax.broadcasted_iota(jnp.int32, (1, CT), 1)
    col_valid = (lane + lc * CT < n).astype(F32)
    lane_block = lane // 16

    def valid_row(i):
        return jnp.where(lr * RT + i < n, col_valid, 0.0)

    for k, ref in enumerate((w_first_ref, w_second_ref)):
        blocks = [ref[a, b] for a in range(3) for b in range(3)]
        wmat[2 * k] = jnp.concatenate(blocks, axis=1)
        flipped = [blocks[8 - t].astype(F32).T.astype(BF16) for t in range(9)]
        wmat[2 * k + 1] = jnp.concatenate(flipped, axis=1)
    for k in range(2):
        gain_b[k] = jnp.broadcast_to(gains_ref[k : k + 1, :], (CT, CH)).T
        shift_b[k] = jnp.broadcast_to(shifts_ref[k : k + 1, :], (CT, CH)).T

    pl.semaphore_wait(barrier, expected)

    def move_tile(k, src, dst, target):
        @pl.when(is_me(target))
        def _():
            pltpu.make_async_copy(src, dst, tile_recv.at[k]).start()

        @pl.when(jnp.logical_not(is_me(target)))
        def _():
            remote(src, dst, tile_send.at[k], tile_recv.at[k], target).start()

    def moved(k, dst):
        wait_bytes(dst, tile_recv.at[k])

    def sent_tile(k, src, target):
        @pl.when(jnp.logical_not(is_me(target)))
        def _():
            wait_bytes(src, tile_send.at[k])

    worker, keeper = place(row, col), holder(lr, lc)
    move_tile(0, pairs_ref, pin, worker)

    def mirror_pack(k, src):
        def step(g, _):
            turned = src[pl.ds(pl.multiple_of(128 * g, 128), 128), :].T
            for b in range(4):
                mir_s[k, b, g] = turned[32 * b : 32 * b + 32].astype(BF16)
            return 0

        lax.fori_loop(0, 16, step, 0)

    def mirror_start(k, tr, tc, where):
        slot = tr % 4
        for b in range(4):
            target = where(4 * tc + b, tr // 4)
            src, dst = mir_s.at[k, b], mir_r.at[k, slot]

            @pl.when(is_me(target))
            def _(src=src, dst=dst):
                pltpu.make_async_copy(src, dst, mir_recv.at[k, slot]).start()

            @pl.when(jnp.logical_not(is_me(target)))
            def _(src=src, dst=dst, target=target, b=b):
                remote(src, dst, mir_send.at[k, b], mir_recv.at[k, slot], target).start()

    def mirror_sent(k, tr, tc, where):
        for b in range(4):
            target = where(4 * tc + b, tr // 4)

            @pl.when(jnp.logical_not(is_me(target)))
            def _(b=b):
                wait_bytes(mir_s.at[k, b], mir_send.at[k, b])

    def mirror_wait(k):
        for s in range(4):
            wait_bytes(mir_r.at[k, s], mir_recv.at[k, s])

    quarter = lax.broadcasted_iota(jnp.int32, (RT, CT), 1) // 32

    def mirror_step(k, g, use):
        got = [mir_r[k, s, g].astype(F32) for s in range(4)]
        for kk in range(4):
            flip = got[kk]
            for s in range(4):
                if s != kk:
                    flip = jnp.where(quarter == s, roll(got[s], (32 * (s - kk)) % 128), flip)
            use(4 * g + kk, flip)

    def to_channels(src, dst):
        def step(g, _):
            block = src[pl.ds(4 * g, 4)].astype(F32).reshape(128, 128)
            dst[pl.ds(pl.multiple_of(128 * g, 128), 128), :] = block
            return 0

        lax.fori_loop(0, 16, step, 0)

    to_channels(cot_ref, S)
    mirror_pack(0, S)

    def keep_rows(ph, value):
        def step(g, _):
            low = jnp.zeros((CH, CT), F32)
            high = jnp.zeros((CH, CT), F32)
            for q in range(8):
                i = 8 * g + q
                v = value(i)
                ext[ph, EDGE + i] = v.astype(BF16)
                here = lane_block == q
                low = jnp.where(here, roll(v, 16 * q) if q else v, low)
                high = jnp.where(here, roll(v, (16 * q + 16) % 128) if q < 7 else v, high)
            lat_s[ph, 0, g] = low.astype(BF16)
            lat_s[ph, 1, g] = high.astype(BF16)
            return 0

        lax.fori_loop(0, 4, step, 0)

    def halo_copies(ph):
        whole, top, bottom = pl.ds(0, 4), pl.ds(0, 2), pl.ds(2, 2)
        mid, head, tail = pl.ds(2, 4), pl.ds(0, 2), pl.ds(6, 2)
        own, got = ext.at[ph], lat_r.at[ph]
        low, high = lat_s.at[ph, 0], lat_s.at[ph, 1]
        plan = (
            (own.at[pl.ds(16, 16)], own.at[pl.ds(48, 16)], (up, lc)),
            (own.at[pl.ds(32, 16)], own.at[pl.ds(0, 16)], (down, lc)),
            (low.at[whole], got.at[1, mid], (lr, left)),
            (high.at[whole], got.at[0, mid], (lr, right)),
            (low.at[top], got.at[1, tail], (up, left)),
            (high.at[top], got.at[0, tail], (up, right)),
            (low.at[bottom], got.at[1, head], (down, left)),
            (high.at[bottom], got.at[0, head], (down, right)),
        )
        return [
            remote(src, dst, halo_send.at[ph, k], halo_recv.at[ph, k], place(*tile))
            for k, (src, dst, tile) in enumerate(plan)
        ]

    def halo_start(ph):
        for copy in halo_copies(ph):
            copy.start()

    def halo_wait(ph):
        for copy in halo_copies(ph):
            copy.wait()
        rows16 = jnp.zeros((EDGE, CH, CT), BF16)
        two = jnp.zeros((2, CH, CT), BF16)
        eight = jnp.zeros((8, CH, CT), BF16)

        @pl.when(lr == 0)
        def _():
            ext[ph, 0:EDGE] = rows16
            lat_r[ph, 0, 0:2] = two
            lat_r[ph, 1, 0:2] = two

        @pl.when(lr == R - 1)
        def _():
            ext[ph, EDGE + RT :] = rows16
            lat_r[ph, 0, 6:8] = two
            lat_r[ph, 1, 6:8] = two

        @pl.when(lc == 0)
        def _():
            lat_r[ph, 0] = eight

        @pl.when(lc == C - 1)
        def _():
            lat_r[ph, 1] = eight

    def spread(ph, d):
        back_by, ahead_by = lane >= d, lane < CT - d

        def step(g, _):
            before = lat_r[ph, 0, g].astype(F32)
            after = lat_r[ph, 1, g].astype(F32)
            for q in range(8):
                e = 8 * g + q
                v = ext[ph, e]
                wide = v.astype(F32)
                low = jnp.where(back_by, roll(wide, d), roll(before, (240 + d - 16 * q) % CT))
                high = jnp.where(ahead_by, roll(wide, CT - d), roll(after, (256 - d - 16 * q) % CT))
                taps[ph, e, 0:CH] = low.astype(BF16)
                taps[ph, e, CH : 2 * CH] = v
                taps[ph, e, 2 * CH :] = high.astype(BF16)
            return 0

        lax.fori_loop(0, 8, step, 0)

    def window(ph, d, i):
        rows = []
        for a in range(3):
            at = i + EDGE + (a - 1) * d
            rows.append(jnp.concatenate([taps[ph, at], taps[ph, at + 1]], axis=1))
        return jnp.concatenate(rows, axis=0)

    def convolve(ph, d, k, use, carry):
        weights = wmat[k]

        def step(t, carry):
            i = 2 * t
            out = jnp.dot(weights, window(ph, d, i), preferred_element_type=F32)
            carry = use(i, out[:, :CT], carry)
            return use(i + 1, out[:, CT:], carry)

        return lax.fori_loop(0, RT // 2, step, carry)

    def to_message(one, two):
        return jnp.sum(jnp.concatenate([one, two], axis=0).T, axis=0, keepdims=True)

    def from_message(msg):
        wide = jnp.broadcast_to(msg, (CT, CT)).T
        return wide[:CH], wide[CH:]

    def sum_start(q, msg):
        mine = m if q % 2 else p
        size = G2 if q % 2 else G1
        ar_s[q] = msg
        ar_r[q, mine] = msg

        def step(k, _):
            t = (mine + k) % size
            target = (2 * t + row % 2, col) if q % 2 else (2 * m + t // C, t % C)
            remote(ar_s.at[q], ar_r.at[q, mine], ar_send_sem.at[q], ar_recv_sem.at[q], target).start()
            return 0

        lax.fori_loop(1, size, step, 0)

    def sum_wait(q):
        size = G2 if q % 2 else G1
        wait_bytes(ar_r.at[q, pl.ds(0, size - 1)], ar_recv_sem.at[q])
        return [ar_r[q, t] for t in range(size)]

    def plain(parts):
        total = parts[0]
        for part in parts[1:]:
            total = total + part
        return total

    def wide_count(number):
        return jnp.full((1, CT), 1.0, F32) * number.astype(F32)

    def pooled(parts, numbers):
        counts = [wide_count(number) for number in numbers]
        total = plain(parts)
        mean = total / jnp.maximum(plain(counts), 1.0)
        apart = jnp.zeros((1, CT), F32)
        for part, number in zip(parts, counts):
            off = part / jnp.maximum(number, 1.0) - mean
            apart = apart + number * off * off
        return jnp.where(lane_row < CH, total, total + roll(apart, CH))

    def extent(start, size):
        return jnp.clip(n - start, 0, size)

    def tile_count(tr, tc):
        return extent(tr * RT, RT) * extent(tc * CT, CT)

    def sums(q):
        sum_start(q + 1, plain(sum_wait(q)))
        return plain(sum_wait(q + 1))

    def norm(q, field, total):
        own = wide_count(tile_count(lr, lc))
        center = jnp.sum(total, axis=1, keepdims=True) / jnp.maximum(own, 1.0)

        def step(i, acc):
            off = (field[i] - center) * valid_row(i)
            return acc + off * off

        spread_sum = lax.fori_loop(0, RT, step, jnp.zeros((CH, CT), F32), unroll=4)
        sum_start(q, to_message(total, spread_sum))
        parts = sum_wait(q)
        numbers = [tile_count(*tile_of(2 * m + t // C, t % C)) for t in range(G1)]
        sum_start(q + 1, pooled(parts, numbers))
        parts = sum_wait(q + 1)
        numbers = [extent(2 * RT * t, 2 * RT) * n for t in range(G2)]
        mean, var = from_message(pooled(parts, numbers) / count)
        return mean, lax.rsqrt(var + EPSILON)

    def grad_taps(k, ph, d, grads):
        w_acc[...] = jnp.zeros(w_acc.shape, F32)

        def step(t, _):
            i = 2 * t
            g = jnp.concatenate([ext[grads, EDGE + i], ext[grads, EDGE + i + 1]], axis=1)
            w_acc[:, : 9 * CH] += lax.dot_general(
                g, window(ph, d, i), (((1,), (1,)), ((), ())), preferred_element_type=F32
            )
            return 0

        lax.fori_loop(0, RT // 2, step, 0)
        for t in range(16):
            r, c = 8 * (t // 2), 384 * (t % 2)
            w_parts[k, t // share, t % share] = w_acc[r : r + 8, c : c + 384]
        w_a[k, p] = w_parts[k, p]

        def send(j, _):
            t = (p + j) % G1
            remote(
                w_parts.at[k, t], w_a.at[k, p], w_send_sem.at[k, 0], w_recv_sem.at[k, 0],
                (2 * m + t // C, t % C),
            ).start()
            return 0

        lax.fori_loop(1, G1, send, 0)

    def grad_taps_across(k):
        wait_bytes(w_a.at[k, pl.ds(0, G1 - 1)], w_recv_sem.at[k, 0])
        total = plain([w_a[k, t] for t in range(G1)])
        w_b_s[k] = total
        w_b[k, m] = total

        def send(j, _):
            t = (m + j) % G2
            remote(
                w_b_s.at[k], w_b.at[k, m], w_send_sem.at[k, 1], w_recv_sem.at[k, 1],
                (2 * t + row % 2, col),
            ).start()
            return 0

        lax.fori_loop(1, G2, send, 0)

    def grad_taps_back(k):
        wait_bytes(w_b.at[k, pl.ds(0, G2 - 1)], w_recv_sem.at[k, 1])
        total = plain([w_b[k, t] for t in range(G2)])
        w_c_s[k] = total
        w_c[k, p] = total

        def send(j, _):
            t = (p + j) % G1
            remote(
                w_c_s.at[k], w_c.at[k, p], w_send_sem.at[k, 2], w_recv_sem.at[k, 2],
                (2 * m + t // C, t % C),
            ).start()
            return 0

        lax.fori_loop(1, G1, send, 0)

    def grad_taps_end(k):
        wait_bytes(w_c.at[k, pl.ds(0, G1 - 1)], w_recv_sem.at[k, 2])
        for t in range(16):
            r, c = 8 * (t // 2), 384 * (t % 2)
            part = w_c[k, t // share, t % share]
            for tap in range(9):
                at = CH * tap - c
                if 0 <= at < 384:
                    gw_ref[k, tap // 3, tap % 3, r : r + 8, :] = part[:, at : at + CH]

    d_one, d_two = dil_ref[0], dil_ref[1]
    moved(0, pin)
    to_channels(pin, S)
    keep_rows(PAIRS, lambda i: S[pl.ds(i, CH, stride=RT), :] * valid_row(i))
    halo_start(PAIRS)
    halo_wait(PAIRS)
    move_tile(1, cot_ref, cin, worker)
    mirror_start(0, row, col, place)
    spread(PAIRS, d_one)

    def keep(field):
        def use(i, out, total):
            field[i] = out
            return total + out * valid_row(i)

        return use

    nothing = jnp.zeros((CH, CT), F32)
    total = convolve(PAIRS, d_one, 0, keep(first), nothing)
    mean_one, inv_one = norm(0, first, total)
    scale_one = inv_one * gain_b[0]
    shift_one = shift_b[0]

    def activate(i):
        level = (first[i] - mean_one) * scale_one + shift_one
        low = jnp.exp(jnp.minimum(level, 0.0))
        valid = valid_row(i)
        slope_one[i] = low * valid
        return jnp.where(level > 0.0, level, low - 1.0) * valid

    keep_rows(ACTIVE, activate)
    halo_start(ACTIVE)

    halo_wait(ACTIVE)
    spread(ACTIVE, d_two)
    total = convolve(ACTIVE, d_two, 2, keep(second), nothing)
    mean_two, inv_two = norm(2, second, total)
    moved(1, cin)
    mirror_wait(0)

    def join_cotangent(g, _):
        def use(c, flip):
            back = (cin[c].astype(F32) + flip) * 0.5
            Sb[pl.ds(pl.multiple_of(RT * c, RT), RT), :] = back

        mirror_step(0, g, use)
        return 0

    lax.fori_loop(0, 16, join_cotangent, 0)
    gain_two = gain_b[1]
    scale_two = inv_two * gain_two
    shift_two = shift_b[1]

    def finish(i, carry):
        p_sum, q_sum = carry
        off = second[i] - mean_two
        before = ext[PAIRS, EDGE + i].astype(F32) + (off * scale_two + shift_two)
        low = jnp.exp(jnp.minimum(before, 0.0))
        valid = valid_row(i)
        S[pl.ds(i, CH, stride=RT), :] = jnp.where(before > 0.0, before, low - 1.0) * valid
        out = Sb[pl.ds(i, CH, stride=RT), :] * valid * low
        outer[i] = out
        scaled = out * gain_two
        return p_sum + scaled, q_sum + scaled * (off * inv_two)

    p_sum, q_sum = lax.fori_loop(0, RT, finish, (nothing, nothing))
    sum_start(4, to_message(p_sum, q_sum))

    def keep_final(g, _):
        block = S[pl.ds(pl.multiple_of(128 * g, 128), 128), :]
        fin_out[pl.ds(4 * g, 4)] = block.reshape(4, RT, CT).astype(BF16)
        return 0

    lax.fori_loop(0, 16, keep_final, 0)
    mirror_pack(1, S)

    p_two, q_two = from_message(sums(4) / count)

    def back_two(i):
        normed = (second[i] - mean_two) * inv_two
        scaled = outer[i] * gain_two
        return valid_row(i) * inv_two * (scaled - p_two - normed * q_two)

    keep_rows(GRAD_TWO, back_two)
    halo_start(GRAD_TWO)
    grad_taps(1, ACTIVE, d_two, GRAD_TWO)
    halo_wait(GRAD_TWO)
    move_tile(2, fin_out, fin_in, keeper)
    mirror_start(1, lr, lc, holder)
    spread(GRAD_TWO, d_two)
    gain_one = gain_b[0]

    def descend(i, out, carry):
        p_sum, q_sum = carry
        up_i = out * slope_one[i]
        inner[i] = up_i
        scaled = up_i * gain_one
        return p_sum + scaled, q_sum + scaled * ((first[i] - mean_one) * inv_one)

    p_sum, q_sum = convolve(GRAD_TWO, d_two, 3, descend, (nothing, nothing))
    sum_start(6, to_message(p_sum, q_sum))
    grad_taps_across(1)
    p_one, q_one = from_message(sums(6) / count)

    def back_one(i):
        normed = (first[i] - mean_one) * inv_one
        scaled = inner[i] * gain_one
        return valid_row(i) * inv_one * (scaled - p_one - normed * q_one)

    keep_rows(GRAD_ONE, back_one)
    halo_start(GRAD_ONE)
    grad_taps(0, PAIRS, d_one, GRAD_ONE)
    grad_taps_back(1)
    halo_wait(GRAD_ONE)
    spread(GRAD_ONE, d_one)

    def lower(i, out, carry):
        S[pl.ds(i, CH, stride=RT), :] = (outer[i] + out) * valid_row(i)
        return carry

    convolve(GRAD_ONE, d_one, 1, lower, 0)

    def keep_grad(g, _):
        block = S[pl.ds(pl.multiple_of(128 * g, 128), 128), :]
        gp_out[pl.ds(4 * g, 4)] = block.reshape(4, RT, CT).astype(BF16)
        return 0

    lax.fori_loop(0, 16, keep_grad, 0)
    move_tile(3, gp_out, gp_ref, keeper)
    grad_taps_across(0)
    moved(2, fin_in)
    mirror_wait(1)

    def join_final(g, _):
        def use(c, flip):
            sym_ref[c] = ((fin_in[c].astype(F32) + flip) * 0.5).astype(BF16)

        mirror_step(1, g, use)
        return 0

    lax.fori_loop(0, 16, join_final, 0)
    grad_taps_back(0)
    grad_taps_end(1)
    grad_taps_end(0)

    sent_tile(0, pin, worker)
    sent_tile(1, cin, worker)
    sent_tile(2, fin_out, keeper)
    sent_tile(3, gp_out, keeper)
    mirror_sent(0, row, col, place)
    mirror_sent(1, lr, lc, holder)
    for q in range(8):
        size = G2 if q % 2 else G1
        wait_bytes(ar_r.at[q, pl.ds(0, size - 1)], ar_send_sem.at[q])
    for k in range(2):
        wait_bytes(w_a.at[k, pl.ds(0, G1 - 1)], w_send_sem.at[k, 0])
        wait_bytes(w_b.at[k, pl.ds(0, G2 - 1)], w_send_sem.at[k, 1])
        wait_bytes(w_c.at[k, pl.ds(0, G1 - 1)], w_send_sem.at[k, 2])
    moved(3, gp_out)


def solution(mesh):
    R, C = mesh.shape["row"], mesh.shape["col"]

    def per_device(pairs, w_first, w_second, gains, shifts, dilations, residue_count, cotangent):
        CH, RT, CT = pairs.shape
        G1, G2 = 2 * C, R // 2
        G, share = max(G1, G2), 16 // G1
        vmem = pl.BlockSpec(memory_space=pltpu.VMEM)
        smem = pl.BlockSpec(memory_space=pltpu.SMEM)
        anywhere = pl.BlockSpec(memory_space=pl.ANY)
        tile = pltpu.VMEM((CH, RT, CT), BF16)
        field = pltpu.VMEM((RT, CH, CT), F32)
        flat = pltpu.VMEM((CH * RT, CT), F32)
        dma = pltpu.SemaphoreType.DMA
        return pl.pallas_call(
            functools.partial(kernel, R, C),
            out_shape=(
                jax.ShapeDtypeStruct((CH, RT, CT), BF16),
                jax.ShapeDtypeStruct((CH, RT, CT), BF16),
                jax.ShapeDtypeStruct((2, 3, 3, CH, CH), F32),
            ),
            in_specs=[smem, smem, anywhere, vmem, vmem, vmem, vmem, vmem],
            out_specs=(vmem, anywhere, vmem),
            scratch_shapes=[
                tile,
                tile,
                tile,
                tile,
                tile,
                pltpu.VMEM((2, 4, 16, RT, CT), BF16),
                pltpu.VMEM((2, 4, 16, RT, CT), BF16),
                pltpu.VMEM((4, RT + 2 * EDGE, CH, CT), BF16),
                pltpu.VMEM((4, 2, 4, CH, CT), BF16),
                pltpu.VMEM((4, 2, 8, CH, CT), BF16),
                pltpu.VMEM((4, RT + 2 * EDGE, 3 * CH, CT), BF16),
                flat,
                flat,
                field,
                field,
                field,
                field,
                field,
                pltpu.VMEM((4, CH, 9 * CH), BF16),
                pltpu.VMEM((2, CH, CT), F32),
                pltpu.VMEM((2, CH, CT), F32),
                pltpu.VMEM((8, 1, CT), F32),
                pltpu.VMEM((8, G, 1, CT), F32),
                pltpu.VMEM((CH, 768), F32),
                pltpu.VMEM((2, G1, share, 8, 384), F32),
                pltpu.VMEM((2, G1, share, 8, 384), F32),
                pltpu.VMEM((2, share, 8, 384), F32),
                pltpu.VMEM((2, G2, share, 8, 384), F32),
                pltpu.VMEM((2, share, 8, 384), F32),
                pltpu.VMEM((2, G1, share, 8, 384), F32),
                dma((4,)),
                dma((4,)),
                dma((4, 8)),
                dma((4, 8)),
                dma((2, 4)),
                dma((2, 4)),
                dma((8,)),
                dma((8,)),
                dma((2, 3)),
                dma((2, 3)),
            ],
            compiler_params=pltpu.CompilerParams(
                collective_id=0, has_side_effects=True, vmem_limit_bytes=56 * 1024 * 1024
            ),
            cost_estimate=pl.CostEstimate(
                flops=6 * 2 * 9 * CH * CH * RT * CT, bytes_accessed=4 * CH * RT * CT, transcendentals=0
            ),
        )(dilations, residue_count, pairs, cotangent, w_first, w_second, gains, shifts)

    in_specs = (P(None, "row", "col"), P(), P(), P(), P(), P(), P(), P(None, "row", "col"))
    out_specs = (P(None, "row", "col"), P(None, "row", "col"), P())
    return jax.shard_map(
        per_device, mesh=mesh, in_specs=in_specs, out_specs=out_specs, check_vma=False
    )
```

time: 1060 us -> 237 us (0.22)
  blocking collectives: 447 us -> 0 us
  waiting for transfers between devices: 316 us -> 0 us
  Pallas kernels: 0 us -> 231 us
  starting transfers between devices: 122 us -> 0 us
  local copies, waits for them, and re-layouts: 83.1 us -> 4 us
  other arithmetic: 31.3 us -> 0 us
  matrix products: 30.3 us -> 0 us
  between operations: 21.4 us -> 1.3 us
    psum x6 -> x0, blocking collectives: 447 us -> none  [channel_sums(): return lax.psum(values, ('row', 'col'))]
    pallas_call x0 -> x1, Pallas kernels: none -> 231 us  [per_device(): pl.pallas_call(functools.partial(kernel, R, C), out_shape=(jax.ShapeDtype...]
    psum x1 -> x0, waiting for transfers between devices: 211 us -> none  [channel_sums(): return lax.psum(values, ('row', 'col'))]
    ppermute x16 -> x0, starting transfers between devices: 77 us -> none  [the longest x8 60.9 us: with_halo(): lax.ppermute(lax.slice_in_dim(block, block.shape[dim] - width, None, axis...]
    ppermute x16 -> x0, waiting for transfers between devices: 71.9 us -> none  [the longest x8 41.3 us: with_halo(): lax.ppermute(lax.slice_in_dim(block, block.shape[dim] - width, None, axis...]
    all_to_all x6 -> x0, starting transfers between devices: 45.3 us -> none  [the longest x2 19.8 us: mirror(): lax.all_to_all(lax.all_to_all(arranged, 'row', split_axis=3, concat_axis=...]
    all_to_all x6 -> x0, waiting for transfers between devices: 32.8 us -> none  [the longest x2 22.8 us: mirror(): lax.all_to_all(arranged, 'row', split_axis=3, concat_axis=3, tiled=True)]
    dot_general x54 -> x0, matrix products: 30.3 us -> none  [the longest x18 12.6 us: convolve_back(): jnp.dot(weights[vertical, lateral].T, portion.reshape(chans, rows * cols)...]
  transfers between devices with their start and end apart: 23 -> 0, of which waited for: 14 -> 0; matrix products, arithmetic and copies ran while one was open for 6% -> 0% of each run, Pallas kernels for 0% -> 0%
where the time goes in v1:
time: 237 us
  Pallas kernels  231 us (97%)
  local copies, waits for them, and re-layouts  4 us (2%)
    pallas_call x1, Pallas kernels, per_device(): pl.pallas_call(functools.partial(kernel, R, C), out_shape=(jax.ShapeDtype...  231 us

profile of v1, /device:TPU:1, one launch (start us, length us, event | category | flops | bytes accessed | tf_op | source)
XLA Modules:
  0.0 236.7 jit_solution(10317247435236537818)
XLA Ops:
  1.3 231.4 %shard_map.103 = (bf16[64,32,128]{2,1,0:T(8,128)(2,1)}, bf16[64,32,128]{2,1,0:T(8,128)(2,1)}, f32[2,3,3,64,64]{4,3,2,1,0:T(8,128)}) custom-call(s32[2]{0:T(128)} %dil_ref.1, s32[1]{0:T(128)S(6)} %copy.14.count_ref, bf16[64,32,128]{2,1,0:T(8,128)(2,1)} %pairs_ref.1, bf16[64,32,128]{2,1,0:T(8,128)(2,1)} %cot_ref.1, bf16[3,3,64,64]{3,2,1,0:T(8,128)(2,1)} %w_first_ref.1, ...), custom_call_target="tpu_custom_call" | custom-call | flops 1811939328 | bytes 1048576 | tf_op jit(solution)/shard_map/pallas_call | solution.py:666
  232.7 0.0 copy-start.1
  232.7 1.9 copy.15
  234.6 0.0 copy-done.1
  234.6 0.0 copy-start
  234.6 0.8 copy.16
  235.4 0.5 copy-done
  235.9 0.8 copy.17
Async XLA Ops:
  232.7 1.9 copy-start.1
  234.6 1.3 copy-start

commit v2 on v1

--- a/solution.py
+++ b/solution.py
@@ -13,6 +13,7 @@
 EPSILON = 1e-05
 EDGE = 16
 PAIRS, ACTIVE, GRAD_TWO, GRAD_ONE = range(4)
+CHIPS = (2, 7, 6, 4, 3, 1, 0, 5)
 
 
 def roll(x, shift):
@@ -40,6 +41,7 @@
     gp_out,
     mir_s,
     mir_r,
+    relayed,
     ext,
     lat_s,
     lat_r,
@@ -71,6 +73,8 @@
     mir_recv,
     ar_send_sem,
     ar_recv_sem,
+    relay_send,
+    relay_recv,
     w_send_sem,
     w_recv_sem,
 ):
@@ -82,13 +86,21 @@
     share = 16 // G1
     m, p = row // 2, (row % 2) * C + col
 
+    chips = CHIPS if C == len(CHIPS) else tuple(range(C))
+
+    def pick(table, k):
+        found = jnp.int32(0)
+        for j, entry in enumerate(table):
+            found = found + jnp.where(k == j, entry, 0)
+        return found
+
     def place(tr, tc):
-        z = (C - tc) % C
+        z = pick(chips, tc)
         return 2 * (tr // 2) + z // half, 2 * (z % half) + tr % 2
 
     def tile_of(r, c):
         z = (r % 2) * half + c // 2
-        return 2 * (r // 2) + c % 2, (C - z) % C
+        return 2 * (r // 2) + c % 2, pick([chips.index(j) for j in range(C)], z)
 
     def holder(tr, tc):
         return tr, tc
@@ -134,14 +146,25 @@
     for tc in (left, lc, right):
         greet(place(across, tc))
     expected = G1 - 1 + G2 - 1 + 3
+    relays = m // 4 == col // 2
+
+    def relay_of(b):
+        mt = 2 * col + b // 2
+        return 2 * mt + row % 2, 2 * (col // 2) + b % 2
+
     for b in range(4):
-        for target in (place(4 * col + b, row // 4), holder(4 * lc + b, lr // 4)):
-            other = jnp.logical_not(is_me(target))
-            expected = expected + other.astype(jnp.int32)
-
-            @pl.when(other)
-            def _(target=target):
-                greet(target)
+        expected = expected + jnp.logical_not(is_me(relay_of(b))).astype(jnp.int32)
+
+    def greet_source(j, _):
+        source = (2 * j + row % 2, m // 2)
+
+        @pl.when(jnp.logical_and(relays, jnp.logical_not(is_me(source))))
+        def _():
+            greet(source)
+
+        return 0
+
+    lax.fori_loop(0, G2, greet_source, 0)
 
     n = count_ref[0]
     count = jnp.full((1, CT), 1.0, F32) * (n.astype(F32) * n.astype(F32))
@@ -162,16 +185,8 @@
         gain_b[k] = jnp.broadcast_to(gains_ref[k : k + 1, :], (CT, CH)).T
         shift_b[k] = jnp.broadcast_to(shifts_ref[k : k + 1, :], (CT, CH)).T
 
-    pl.semaphore_wait(barrier, expected)
-
     def move_tile(k, src, dst, target):
-        @pl.when(is_me(target))
-        def _():
-            pltpu.make_async_copy(src, dst, tile_recv.at[k]).start()
-
-        @pl.when(jnp.logical_not(is_me(target)))
-        def _():
-            remote(src, dst, tile_send.at[k], tile_recv.at[k], target).start()
+        either(src, dst, tile_send.at[k], tile_recv.at[k], target)
 
     def moved(k, dst):
         wait_bytes(dst, tile_recv.at[k])
@@ -182,7 +197,7 @@
             wait_bytes(src, tile_send.at[k])
 
     worker, keeper = place(row, col), holder(lr, lc)
-    move_tile(0, pairs_ref, pin, worker)
+    lower_half, upper_half = pl.ds(0, CH // 2), pl.ds(CH // 2, CH // 2)
 
     def mirror_pack(k, src):
         def step(g, _):
@@ -193,27 +208,64 @@
 
         lax.fori_loop(0, 16, step, 0)
 
-    def mirror_start(k, tr, tc, where):
-        slot = tr % 4
+    def either(src, dst, send, recv, target):
+        @pl.when(is_me(target))
+        def _():
+            pltpu.make_async_copy(src, dst, recv).start()
+
+        @pl.when(jnp.logical_not(is_me(target)))
+        def _():
+            remote(src, dst, send, recv, target).start()
+
+    def cross_start():
         for b in range(4):
-            target = where(4 * tc + b, tr // 4)
-            src, dst = mir_s.at[k, b], mir_r.at[k, slot]
-
-            @pl.when(is_me(target))
-            def _(src=src, dst=dst):
-                pltpu.make_async_copy(src, dst, mir_recv.at[k, slot]).start()
-
-            @pl.when(jnp.logical_not(is_me(target)))
-            def _(src=src, dst=dst, target=target, b=b):
-                remote(src, dst, mir_send.at[k, b], mir_recv.at[k, slot], target).start()
-
-    def mirror_sent(k, tr, tc, where):
+            either(mir_s.at[0, b], relayed.at[m], mir_send.at[0, b], relay_recv.at[m], relay_of(b))
+
+    def cross_target(j):
+        return place(2 * m + col % 2, j // 2)
+
+    def cross_on(first, last):
+        def step(j, _):
+            @pl.when(relays)
+            def _():
+                wait_bytes(relayed.at[j], relay_recv.at[j])
+                slot = 2 * (j % 2) + row % 2
+                either(
+                    relayed.at[j], mir_r.at[0, slot], relay_send.at[j], mir_recv.at[0, slot], cross_target(j)
+                )
+
+            return 0
+
+        lax.fori_loop(first, last, step, 0)
+
+    def cross_sent():
         for b in range(4):
-            target = where(4 * tc + b, tr // 4)
-
-            @pl.when(jnp.logical_not(is_me(target)))
+
+            @pl.when(jnp.logical_not(is_me(relay_of(b))))
             def _(b=b):
-                wait_bytes(mir_s.at[k, b], mir_send.at[k, b])
+                wait_bytes(mir_s.at[0, b], mir_send.at[0, b])
+
+        def step(j, _):
+            @pl.when(jnp.logical_and(relays, jnp.logical_not(is_me(cross_target(j)))))
+            def _():
+                wait_bytes(relayed.at[j], relay_send.at[j])
+
+            return 0
+
+        lax.fori_loop(0, G2, step, 0)
+
+    def mirror_block(b):
+        either(
+            mir_s.at[1, b], mir_r.at[1, lr % 4], mir_send.at[1, b], mir_recv.at[1, lr % 4],
+            holder(4 * lc + b, lr // 4),
+        )
+
+    def mirror_sent():
+        for b in range(4):
+
+            @pl.when(jnp.logical_not(is_me(holder(4 * lc + b, lr // 4))))
+            def _(b=b):
+                wait_bytes(mir_s.at[1, b], mir_send.at[1, b])
 
     def mirror_wait(k):
         for s in range(4):
@@ -240,6 +292,9 @@
 
     to_channels(cot_ref, S)
     mirror_pack(0, S)
+    pl.semaphore_wait(barrier, expected)
+    move_tile(0, pairs_ref, pin, worker)
+    cross_start()
 
     def keep_rows(ph, value):
         def step(g, _):
@@ -397,11 +452,14 @@
     def tile_count(tr, tc):
         return extent(tr * RT, RT) * extent(tc * CT, CT)
 
-    def sums(q):
+    def sums(q, message, beside_one, beside_two):
+        sum_start(q, message)
+        beside_one()
         sum_start(q + 1, plain(sum_wait(q)))
+        beside_two()
         return plain(sum_wait(q + 1))
 
-    def norm(q, field, total):
+    def norm(q, field, total, beside_one, beside_two):
         own = wide_count(tile_count(lr, lc))
         center = jnp.sum(total, axis=1, keepdims=True) / jnp.maximum(own, 1.0)
 
@@ -411,9 +469,11 @@
 
         spread_sum = lax.fori_loop(0, RT, step, jnp.zeros((CH, CT), F32), unroll=4)
         sum_start(q, to_message(total, spread_sum))
+        beside_one()
         parts = sum_wait(q)
         numbers = [tile_count(*tile_of(2 * m + t // C, t % C)) for t in range(G1)]
         sum_start(q + 1, pooled(parts, numbers))
+        beside_two()
         parts = sum_wait(q + 1)
         numbers = [extent(2 * RT * t, 2 * RT) * n for t in range(G2)]
         mean, var = from_message(pooled(parts, numbers) / count)
@@ -493,9 +553,8 @@
     to_channels(pin, S)
     keep_rows(PAIRS, lambda i: S[pl.ds(i, CH, stride=RT), :] * valid_row(i))
     halo_start(PAIRS)
+    move_tile(1, cot_ref, cin, worker)
     halo_wait(PAIRS)
-    move_tile(1, cot_ref, cin, worker)
-    mirror_start(0, row, col, place)
     spread(PAIRS, d_one)
 
     def keep(field):
@@ -507,7 +566,9 @@
 
     nothing = jnp.zeros((CH, CT), F32)
     total = convolve(PAIRS, d_one, 0, keep(first), nothing)
-    mean_one, inv_one = norm(0, first, total)
+    mean_one, inv_one = norm(
+        0, first, total, lambda: cross_on(0, G2 // 2), lambda: cross_on(G2 // 2, G2)
+    )
     scale_one = inv_one * gain_b[0]
     shift_one = shift_b[0]
 
@@ -524,7 +585,7 @@
     halo_wait(ACTIVE)
     spread(ACTIVE, d_two)
     total = convolve(ACTIVE, d_two, 2, keep(second), nothing)
-    mean_two, inv_two = norm(2, second, total)
+    mean_two, inv_two = norm(2, second, total, lambda: None, lambda: None)
     moved(1, cin)
     mirror_wait(0)
 
@@ -554,17 +615,22 @@
         return p_sum + scaled, q_sum + scaled * (off * inv_two)
 
     p_sum, q_sum = lax.fori_loop(0, RT, finish, (nothing, nothing))
-    sum_start(4, to_message(p_sum, q_sum))
-
-    def keep_final(g, _):
-        block = S[pl.ds(pl.multiple_of(128 * g, 128), 128), :]
-        fin_out[pl.ds(4 * g, 4)] = block.reshape(4, RT, CT).astype(BF16)
-        return 0
-
-    lax.fori_loop(0, 16, keep_final, 0)
-    mirror_pack(1, S)
-
-    p_two, q_two = from_message(sums(4) / count)
+
+    def send_final():
+        def keep_final(g, _):
+            block = S[pl.ds(pl.multiple_of(128 * g, 128), 128), :]
+            fin_out[pl.ds(4 * g, 4)] = block.reshape(4, RT, CT).astype(BF16)
+            return 0
+
+        lax.fori_loop(0, 16, keep_final, 0)
+        move_tile(2, fin_out.at[lower_half], fin_in.at[lower_half], keeper)
+        mirror_pack(1, S)
+
+    def send_final_rest():
+        move_tile(3, fin_out.at[upper_half], fin_in.at[upper_half], keeper)
+
+    totals = sums(4, to_message(p_sum, q_sum), send_final, send_final_rest)
+    p_two, q_two = from_message(totals / count)
 
     def back_two(i):
         normed = (second[i] - mean_two) * inv_two
@@ -573,10 +639,10 @@
 
     keep_rows(GRAD_TWO, back_two)
     halo_start(GRAD_TWO)
+    mirror_block(0)
     grad_taps(1, ACTIVE, d_two, GRAD_TWO)
     halo_wait(GRAD_TWO)
-    move_tile(2, fin_out, fin_in, keeper)
-    mirror_start(1, lr, lc, holder)
+    mirror_block(1)
     spread(GRAD_TWO, d_two)
     gain_one = gain_b[0]
 
@@ -588,9 +654,13 @@
         return p_sum + scaled, q_sum + scaled * ((first[i] - mean_one) * inv_one)
 
     p_sum, q_sum = convolve(GRAD_TWO, d_two, 3, descend, (nothing, nothing))
-    sum_start(6, to_message(p_sum, q_sum))
-    grad_taps_across(1)
-    p_one, q_one = from_message(sums(6) / count)
+
+    def beside_inner():
+        mirror_block(2)
+        grad_taps_across(1)
+
+    totals = sums(6, to_message(p_sum, q_sum), beside_inner, lambda: mirror_block(3))
+    p_one, q_one = from_message(totals / count)
 
     def back_one(i):
         normed = (first[i] - mean_one) * inv_one
@@ -616,9 +686,10 @@
         return 0
 
     lax.fori_loop(0, 16, keep_grad, 0)
-    move_tile(3, gp_out, gp_ref, keeper)
+    move_tile(4, gp_out.at[lower_half], gp_ref.at[lower_half], keeper)
     grad_taps_across(0)
-    moved(2, fin_in)
+    moved(2, fin_in.at[lower_half])
+    moved(3, fin_in.at[upper_half])
     mirror_wait(1)
 
     def join_final(g, _):
@@ -630,15 +701,16 @@
 
     lax.fori_loop(0, 16, join_final, 0)
     grad_taps_back(0)
+    move_tile(5, gp_out.at[upper_half], gp_ref.at[upper_half], keeper)
     grad_taps_end(1)
     grad_taps_end(0)
 
     sent_tile(0, pin, worker)
     sent_tile(1, cin, worker)
-    sent_tile(2, fin_out, keeper)
-    sent_tile(3, gp_out, keeper)
-    mirror_sent(0, row, col, place)
-    mirror_sent(1, lr, lc, holder)
+    for k in (2, 3, 4, 5):
+        sent_tile(k, fin_out.at[lower_half], keeper)
+    cross_sent()
+    mirror_sent()
     for q in range(8):
         size = G2 if q % 2 else G1
         wait_bytes(ar_r.at[q, pl.ds(0, size - 1)], ar_send_sem.at[q])
@@ -646,7 +718,8 @@
         wait_bytes(w_a.at[k, pl.ds(0, G1 - 1)], w_send_sem.at[k, 0])
         wait_bytes(w_b.at[k, pl.ds(0, G2 - 1)], w_send_sem.at[k, 1])
         wait_bytes(w_c.at[k, pl.ds(0, G1 - 1)], w_send_sem.at[k, 2])
-    moved(3, gp_out)
+    moved(4, gp_out.at[lower_half])
+    moved(5, gp_out.at[upper_half])
 
 
 def solution(mesh):
@@ -680,6 +753,7 @@
                 tile,
                 pltpu.VMEM((2, 4, 16, RT, CT), BF16),
                 pltpu.VMEM((2, 4, 16, RT, CT), BF16),
+                pltpu.VMEM((G2, 16, RT, CT), BF16),
                 pltpu.VMEM((4, RT + 2 * EDGE, CH, CT), BF16),
                 pltpu.VMEM((4, 2, 4, CH, CT), BF16),
                 pltpu.VMEM((4, 2, 8, CH, CT), BF16),
@@ -703,14 +777,16 @@
                 pltpu.VMEM((2, G2, share, 8, 384), F32),
                 pltpu.VMEM((2, share, 8, 384), F32),
                 pltpu.VMEM((2, G1, share, 8, 384), F32),
-                dma((4,)),
-                dma((4,)),
+                dma((6,)),
+                dma((6,)),
                 dma((4, 8)),
                 dma((4, 8)),
                 dma((2, 4)),
                 dma((2, 4)),
                 dma((8,)),
                 dma((8,)),
+                dma((G2,)),
+                dma((G2,)),
                 dma((2, 3)),
                 dma((2, 3)),
             ],

time: 237 us -> 205 us (0.86)
  Pallas kernels: 231 us -> 199 us
    pallas_call x1, Pallas kernels: 231 us -> 199 us  [per_device(): pl.pallas_call(functools.partial(kernel, R, C), out_shape=(jax.ShapeDtype...]
where the time goes in v2:
time: 205 us; the launch traced here: 204 us
  Pallas kernels  199 us (97%)
  local copies, waits for them, and re-layouts  4 us (2%)
    pallas_call x1, Pallas kernels, per_device(): pl.pallas_call(functools.partial(kernel, R, C), out_shape=(jax.ShapeDtype...  199 us

profile of v2, /device:TPU:1, one launch (start us, length us, event | category | flops | bytes accessed | tf_op | source)
XLA Modules:
  0.0 204.5 jit_solution(1036260729242456017)
XLA Ops:
  1.3 199.2 %shard_map.103 = (bf16[64,32,128]{2,1,0:T(8,128)(2,1)}, bf16[64,32,128]{2,1,0:T(8,128)(2,1)}, f32[2,3,3,64,64]{4,3,2,1,0:T(8,128)}) custom-call(s32[2]{0:T(128)} %dil_ref.1, s32[1]{0:T(128)S(6)} %copy.14.count_ref, bf16[64,32,128]{2,1,0:T(8,128)(2,1)} %pairs_ref.1, bf16[64,32,128]{2,1,0:T(8,128)(2,1)} %cot_ref.1, bf16[3,3,64,64]{3,2,1,0:T(8,128)(2,1)} %w_first_ref.1, ...), custom_call_target="tpu_custom_call" | custom-call | flops 1811939328 | bytes 1048576 | tf_op jit(solution)/shard_map/pallas_call | solution.py:739
  200.5 0.0 copy-start.1
  200.5 1.9 copy.15
  202.4 0.0 copy-done.1
  202.4 0.0 copy-start
  202.4 0.8 copy.16
  203.2 0.5 copy-done
  203.7 0.8 copy.17
Async XLA Ops:
  200.5 1.9 copy-start.1
  202.4 1.3 copy-start

commit v3 on v2

--- a/solution.py
+++ b/solution.py
@@ -13,6 +13,7 @@
 EPSILON = 1e-05
 EDGE = 16
 PAIRS, ACTIVE, GRAD_TWO, GRAD_ONE = range(4)
+FIRST, SECOND, OUTER, INNER = range(4)
 CHIPS = (2, 7, 6, 4, 3, 1, 0, 5)
 
 
@@ -48,11 +49,10 @@
     taps,
     S,
     Sb,
-    first,
-    second,
+    wide,
+    beside_s,
+    beside_r,
     slope_one,
-    outer,
-    inner,
     wmat,
     gain_b,
     shift_b,
@@ -83,7 +83,7 @@
     col = lax.axis_index("col")
     half = C // 2
     G1, G2 = 2 * C, R // 2
-    share = 16 // G1
+    share = 16 // G2
     m, p = row // 2, (row % 2) * C + col
 
     chips = CHIPS if C == len(CHIPS) else tuple(range(C))
@@ -176,6 +176,16 @@
     def valid_row(i):
         return jnp.where(lr * RT + i < n, col_valid, 0.0)
 
+    def valid_wide(e):
+        at = lr * RT + e - EDGE
+        return jnp.where(jnp.logical_and(at >= 0, at < n), col_valid, 0.0)
+
+    def valid_beside(side, g):
+        at_row = lr * RT + 8 * g - EDGE + lane_block
+        at_col = lc * CT + (CT if side else -EDGE) + lane % 16
+        inside = jnp.logical_and(at_row >= 0, at_row < n)
+        return jnp.where(jnp.logical_and(inside, jnp.logical_and(at_col >= 0, at_col < n)), 1.0, 0.0)
+
     for k, ref in enumerate((w_first_ref, w_second_ref)):
         blocks = [ref[a, b] for a in range(3) for b in range(3)]
         wmat[2 * k] = jnp.concatenate(blocks, axis=1)
@@ -254,9 +264,11 @@
 
         lax.fori_loop(0, G2, step, 0)
 
-    def mirror_block(b):
+    def mirror_half(b, h):
+        part, slot = pl.ds(8 * h, 8), lr % 4
         either(
-            mir_s.at[1, b], mir_r.at[1, lr % 4], mir_send.at[1, b], mir_recv.at[1, lr % 4],
+            mir_s.at[1, b, part], mir_r.at[1, slot, part],
+            mir_send.at[1, 2 * b + h], mir_recv.at[1, 2 * slot + h],
             holder(4 * lc + b, lr // 4),
         )
 
@@ -265,11 +277,16 @@
 
             @pl.when(jnp.logical_not(is_me(holder(4 * lc + b, lr // 4))))
             def _(b=b):
-                wait_bytes(mir_s.at[1, b], mir_send.at[1, b])
+                for h in range(2):
+                    wait_bytes(mir_s.at[1, b, pl.ds(8 * h, 8)], mir_send.at[1, 2 * b + h])
 
     def mirror_wait(k):
         for s in range(4):
-            wait_bytes(mir_r.at[k, s], mir_recv.at[k, s])
+            if k == 0:
+                wait_bytes(mir_r.at[k, s], mir_recv.at[k, s])
+            else:
+                for h in range(2):
+                    wait_bytes(mir_r.at[k, s, pl.ds(8 * h, 8)], mir_recv.at[k, 2 * s + h])
 
     quarter = lax.broadcasted_iota(jnp.int32, (RT, CT), 1) // 32
 
@@ -296,28 +313,24 @@
     move_tile(0, pairs_ref, pin, worker)
     cross_start()
 
-    def keep_rows(ph, value):
+    def pack_columns(value, put):
         def step(g, _):
             low = jnp.zeros((CH, CT), F32)
             high = jnp.zeros((CH, CT), F32)
             for q in range(8):
-                i = 8 * g + q
-                v = value(i)
-                ext[ph, EDGE + i] = v.astype(BF16)
+                v = value(8 * g + q)
                 here = lane_block == q
                 low = jnp.where(here, roll(v, 16 * q) if q else v, low)
                 high = jnp.where(here, roll(v, (16 * q + 16) % 128) if q < 7 else v, high)
-            lat_s[ph, 0, g] = low.astype(BF16)
-            lat_s[ph, 1, g] = high.astype(BF16)
+            put(g, low, high)
             return 0
 
         lax.fori_loop(0, 4, step, 0)
 
-    def halo_copies(ph):
+    def pairs_copies():
+        own, low, high, got = ext, lat_s.at[0], lat_s.at[1], lat_r
         whole, top, bottom = pl.ds(0, 4), pl.ds(0, 2), pl.ds(2, 2)
         mid, head, tail = pl.ds(2, 4), pl.ds(0, 2), pl.ds(6, 2)
-        own, got = ext.at[ph], lat_r.at[ph]
-        low, high = lat_s.at[ph, 0], lat_s.at[ph, 1]
         plan = (
             (own.at[pl.ds(16, 16)], own.at[pl.ds(48, 16)], (up, lc)),
             (own.at[pl.ds(32, 16)], own.at[pl.ds(0, 16)], (down, lc)),
@@ -329,16 +342,68 @@
             (high.at[bottom], got.at[0, head], (down, right)),
         )
         return [
-            remote(src, dst, halo_send.at[ph, k], halo_recv.at[ph, k], place(*tile))
+            remote(src, dst, halo_send.at[0, k], halo_recv.at[0, k], place(*tile))
             for k, (src, dst, tile) in enumerate(plan)
         ]
 
-    def halo_start(ph):
-        for copy in halo_copies(ph):
+    def field_copies(f):
+        own, got = wide.at[f], beside_r.at[f]
+        plan = (
+            (own.at[pl.ds(16, 16)], own.at[pl.ds(48, 16)], (up, lc)),
+            (own.at[pl.ds(32, 16)], own.at[pl.ds(0, 16)], (down, lc)),
+            (beside_s.at[f, 0], got.at[1, pl.ds(2, 4)], (lr, left)),
+            (beside_s.at[f, 1], got.at[0, pl.ds(2, 4)], (lr, right)),
+            (got.at[0, pl.ds(2, 2)], got.at[0, pl.ds(6, 2)], (up, lc)),
+            (got.at[1, pl.ds(2, 2)], got.at[1, pl.ds(6, 2)], (up, lc)),
+            (got.at[0, pl.ds(4, 2)], got.at[0, pl.ds(0, 2)], (down, lc)),
+            (got.at[1, pl.ds(4, 2)], got.at[1, pl.ds(0, 2)], (down, lc)),
+        )
+        return [
+            remote(src, dst, halo_send.at[1 + f, k], halo_recv.at[1 + f, k], place(*tile))
+            for k, (src, dst, tile) in enumerate(plan)
+        ]
+
+    def rows_start(f):
+        for copy in field_copies(f)[:2]:
             copy.start()
 
-    def halo_wait(ph):
-        for copy in halo_copies(ph):
+    def columns_start(f):
+        def put(g, low, high):
+            beside_s[f, 0, g] = low
+            beside_s[f, 1, g] = high
+
+        pack_columns(lambda i: wide[f, EDGE + i], put)
+        for copy in field_copies(f)[2:4]:
+            copy.start()
+
+    def corners_start(f):
+        copies = field_copies(f)
+        for copy in copies[2:4]:
+            copy.wait()
+        for copy in copies[4:]:
+            copy.start()
+
+    def field_wait(f):
+        copies = field_copies(f)
+        for copy in copies[:2] + copies[4:]:
+            copy.wait()
+
+    def pairs_start():
+        def value(i):
+            v = S[pl.ds(i, CH, stride=RT), :] * valid_row(i)
+            ext[EDGE + i] = v.astype(BF16)
+            return v
+
+        def put(g, low, high):
+            lat_s[0, g] = low.astype(BF16)
+            lat_s[1, g] = high.astype(BF16)
+
+        pack_columns(value, put)
+        for copy in pairs_copies():
+            copy.start()
+
+    def pairs_wait():
+        for copy in pairs_copies():
             copy.wait()
         rows16 = jnp.zeros((EDGE, CH, CT), BF16)
         two = jnp.zeros((2, CH, CT), BF16)
@@ -346,42 +411,43 @@
 
         @pl.when(lr == 0)
         def _():
-            ext[ph, 0:EDGE] = rows16
-            lat_r[ph, 0, 0:2] = two
-            lat_r[ph, 1, 0:2] = two
+            ext[0:EDGE] = rows16
+            lat_r[0, 0:2] = two
+            lat_r[1, 0:2] = two
 
         @pl.when(lr == R - 1)
         def _():
-            ext[ph, EDGE + RT :] = rows16
-            lat_r[ph, 0, 6:8] = two
-            lat_r[ph, 1, 6:8] = two
+            ext[EDGE + RT :] = rows16
+            lat_r[0, 6:8] = two
+            lat_r[1, 6:8] = two
 
         @pl.when(lc == 0)
         def _():
-            lat_r[ph, 0] = eight
+            lat_r[0] = eight
 
         @pl.when(lc == C - 1)
         def _():
-            lat_r[ph, 1] = eight
-
-    def spread(ph, d):
+            lat_r[1] = eight
+
+    def spread(ph, d, value, beside):
         back_by, ahead_by = lane >= d, lane < CT - d
 
         def step(g, _):
-            before = lat_r[ph, 0, g].astype(F32)
-            after = lat_r[ph, 1, g].astype(F32)
+            before, after = beside(0, g), beside(1, g)
             for q in range(8):
                 e = 8 * g + q
-                v = ext[ph, e]
-                wide = v.astype(F32)
-                low = jnp.where(back_by, roll(wide, d), roll(before, (240 + d - 16 * q) % CT))
-                high = jnp.where(ahead_by, roll(wide, CT - d), roll(after, (256 - d - 16 * q) % CT))
+                v = value(e)
+                low = jnp.where(back_by, roll(v, d), roll(before, (240 + d - 16 * q) % CT))
+                high = jnp.where(ahead_by, roll(v, CT - d), roll(after, (256 - d - 16 * q) % CT))
                 taps[ph, e, 0:CH] = low.astype(BF16)
-                taps[ph, e, CH : 2 * CH] = v
+                taps[ph, e, CH : 2 * CH] = v.astype(BF16)
                 taps[ph, e, 2 * CH :] = high.astype(BF16)
             return 0
 
         lax.fori_loop(0, 8, step, 0)
+
+    def own_row(ph, i):
+        return taps[ph, EDGE + i, CH : 2 * CH]
 
     def window(ph, d, i):
         rows = []
@@ -399,7 +465,7 @@
             carry = use(i, out[:, :CT], carry)
             return use(i + 1, out[:, CT:], carry)
 
-        return lax.fori_loop(0, RT // 2, step, carry)
+        return lax.fori_loop(0, RT // 2, step, carry, unroll=4)
 
     def to_message(one, two):
         return jnp.sum(jnp.concatenate([one, two], axis=0).T, axis=0, keepdims=True)
@@ -464,7 +530,7 @@
         center = jnp.sum(total, axis=1, keepdims=True) / jnp.maximum(own, 1.0)
 
         def step(i, acc):
-            off = (field[i] - center) * valid_row(i)
+            off = (wide[field, EDGE + i] - center) * valid_row(i)
             return acc + off * off
 
         spread_sum = lax.fori_loop(0, RT, step, jnp.zeros((CH, CT), F32), unroll=4)
@@ -483,63 +549,64 @@
         w_acc[...] = jnp.zeros(w_acc.shape, F32)
 
         def step(t, _):
-            i = 2 * t
-            g = jnp.concatenate([ext[grads, EDGE + i], ext[grads, EDGE + i + 1]], axis=1)
+            i = 4 * t
+            g = jnp.concatenate([own_row(grads, i + j) for j in range(4)], axis=1)
+            around = jnp.concatenate([window(ph, d, i), window(ph, d, i + 2)], axis=1)
             w_acc[:, : 9 * CH] += lax.dot_general(
-                g, window(ph, d, i), (((1,), (1,)), ((), ())), preferred_element_type=F32
+                g, around, (((1,), (1,)), ((), ())), preferred_element_type=F32
             )
             return 0
 
-        lax.fori_loop(0, RT // 2, step, 0)
+        lax.fori_loop(0, RT // 4, step, 0, unroll=2)
         for t in range(16):
             r, c = 8 * (t // 2), 384 * (t % 2)
             w_parts[k, t // share, t % share] = w_acc[r : r + 8, c : c + 384]
-        w_a[k, p] = w_parts[k, p]
+        w_a[k, m] = w_parts[k, m]
+
+        def send(j, _):
+            t = (m + j) % G2
+            remote(
+                w_parts.at[k, t], w_a.at[k, m], w_send_sem.at[k, 0], w_recv_sem.at[k, 0],
+                (2 * t + row % 2, col),
+            ).start()
+            return 0
+
+        lax.fori_loop(1, G2, send, 0)
+
+    def grad_taps_across(k):
+        wait_bytes(w_a.at[k, pl.ds(0, G2 - 1)], w_recv_sem.at[k, 0])
+        total = plain([w_a[k, t] for t in range(G2)])
+        w_b_s[k] = total
+        w_b[k, p] = total
 
         def send(j, _):
             t = (p + j) % G1
             remote(
-                w_parts.at[k, t], w_a.at[k, p], w_send_sem.at[k, 0], w_recv_sem.at[k, 0],
+                w_b_s.at[k], w_b.at[k, p], w_send_sem.at[k, 1], w_recv_sem.at[k, 1],
                 (2 * m + t // C, t % C),
             ).start()
             return 0
 
         lax.fori_loop(1, G1, send, 0)
 
-    def grad_taps_across(k):
-        wait_bytes(w_a.at[k, pl.ds(0, G1 - 1)], w_recv_sem.at[k, 0])
-        total = plain([w_a[k, t] for t in range(G1)])
-        w_b_s[k] = total
-        w_b[k, m] = total
+    def grad_taps_back(k):
+        wait_bytes(w_b.at[k, pl.ds(0, G1 - 1)], w_recv_sem.at[k, 1])
+        total = plain([w_b[k, t] for t in range(G1)])
+        w_c_s[k] = total
+        w_c[k, m] = total
 
         def send(j, _):
             t = (m + j) % G2
             remote(
-                w_b_s.at[k], w_b.at[k, m], w_send_sem.at[k, 1], w_recv_sem.at[k, 1],
+                w_c_s.at[k], w_c.at[k, m], w_send_sem.at[k, 2], w_recv_sem.at[k, 2],
                 (2 * t + row % 2, col),
             ).start()
             return 0
 
         lax.fori_loop(1, G2, send, 0)
 
-    def grad_taps_back(k):
-        wait_bytes(w_b.at[k, pl.ds(0, G2 - 1)], w_recv_sem.at[k, 1])
-        total = plain([w_b[k, t] for t in range(G2)])
-        w_c_s[k] = total
-        w_c[k, p] = total
-
-        def send(j, _):
-            t = (p + j) % G1
-            remote(
-                w_c_s.at[k], w_c.at[k, p], w_send_sem.at[k, 2], w_recv_sem.at[k, 2],
-                (2 * m + t // C, t % C),
-            ).start()
-            return 0
-
-        lax.fori_loop(1, G1, send, 0)
-
     def grad_taps_end(k):
-        wait_bytes(w_c.at[k, pl.ds(0, G1 - 1)], w_recv_sem.at[k, 2])
+        wait_bytes(w_c.at[k, pl.ds(0, G2 - 1)], w_recv_sem.at[k, 2])
         for t in range(16):
             r, c = 8 * (t // 2), 384 * (t % 2)
             part = w_c[k, t // share, t % share]
@@ -551,72 +618,90 @@
     d_one, d_two = dil_ref[0], dil_ref[1]
     moved(0, pin)
     to_channels(pin, S)
-    keep_rows(PAIRS, lambda i: S[pl.ds(i, CH, stride=RT), :] * valid_row(i))
-    halo_start(PAIRS)
+    pairs_start()
     move_tile(1, cot_ref, cin, worker)
-    halo_wait(PAIRS)
-    spread(PAIRS, d_one)
-
-    def keep(field):
+    pairs_wait()
+    spread(
+        PAIRS, d_one, lambda e: ext[e].astype(F32), lambda side, g: lat_r[side, g].astype(F32)
+    )
+
+
+    def keep(f):
         def use(i, out, total):
-            field[i] = out
+            wide[f, EDGE + i] = out
             return total + out * valid_row(i)
 
         return use
 
     nothing = jnp.zeros((CH, CT), F32)
-    total = convolve(PAIRS, d_one, 0, keep(first), nothing)
-    mean_one, inv_one = norm(
-        0, first, total, lambda: cross_on(0, G2 // 2), lambda: cross_on(G2 // 2, G2)
-    )
+    total = convolve(PAIRS, d_one, 0, keep(FIRST), nothing)
+    rows_start(FIRST)
+
+    def beside_first():
+        columns_start(FIRST)
+        cross_on(0 * G2 // 16, 10 * G2 // 16)
+
+    mean_one, inv_one = norm(0, FIRST, total, beside_first, lambda: corners_start(FIRST))
     scale_one = inv_one * gain_b[0]
     shift_one = shift_b[0]
 
-    def activate(i):
-        level = (first[i] - mean_one) * scale_one + shift_one
+    def activate(raw, valid):
+        level = (raw - mean_one) * scale_one + shift_one
         low = jnp.exp(jnp.minimum(level, 0.0))
-        valid = valid_row(i)
-        slope_one[i] = low * valid
-        return jnp.where(level > 0.0, level, low - 1.0) * valid
-
-    keep_rows(ACTIVE, activate)
-    halo_start(ACTIVE)
-
-    halo_wait(ACTIVE)
-    spread(ACTIVE, d_two)
-    total = convolve(ACTIVE, d_two, 2, keep(second), nothing)
-    mean_two, inv_two = norm(2, second, total, lambda: None, lambda: None)
-    moved(1, cin)
-    mirror_wait(0)
-
-    def join_cotangent(g, _):
-        def use(c, flip):
-            back = (cin[c].astype(F32) + flip) * 0.5
-            Sb[pl.ds(pl.multiple_of(RT * c, RT), RT), :] = back
-
-        mirror_step(0, g, use)
-        return 0
-
-    lax.fori_loop(0, 16, join_cotangent, 0)
+        return jnp.where(level > 0.0, level, low - 1.0) * valid, low * valid
+
+    def active_row(e):
+        active, slope = activate(wide[FIRST, e], valid_wide(e))
+        slope_one[e] = slope
+        return active
+
+    def active_beside(side, g):
+        return activate(beside_r[FIRST, side, g], valid_beside(side, g))[0]
+
+    field_wait(FIRST)
+    spread(ACTIVE, d_two, active_row, active_beside)
+    cross_on(10 * G2 // 16, 16 * G2 // 16)
+    total = convolve(ACTIVE, d_two, 2, keep(SECOND), nothing)
+    rows_start(SECOND)
+
+    def join_cotangent():
+        corners_start(SECOND)
+        moved(1, cin)
+        mirror_wait(0)
+
+        def join(g, _):
+            def use(c, flip):
+                back = (cin[c].astype(F32) + flip) * 0.5
+                Sb[pl.ds(pl.multiple_of(RT * c, RT), RT), :] = back
+
+            mirror_step(0, g, use)
+            return 0
+
+        lax.fori_loop(0, 16, join, 0)
+
+    mean_two, inv_two = norm(2, SECOND, total, lambda: columns_start(SECOND), join_cotangent)
     gain_two = gain_b[1]
     scale_two = inv_two * gain_two
     shift_two = shift_b[1]
 
     def finish(i, carry):
         p_sum, q_sum = carry
-        off = second[i] - mean_two
-        before = ext[PAIRS, EDGE + i].astype(F32) + (off * scale_two + shift_two)
+        off = wide[SECOND, EDGE + i] - mean_two
+        before = own_row(PAIRS, i).astype(F32) + (off * scale_two + shift_two)
         low = jnp.exp(jnp.minimum(before, 0.0))
         valid = valid_row(i)
         S[pl.ds(i, CH, stride=RT), :] = jnp.where(before > 0.0, before, low - 1.0) * valid
         out = Sb[pl.ds(i, CH, stride=RT), :] * valid * low
-        outer[i] = out
+        wide[OUTER, EDGE + i] = out
         scaled = out * gain_two
         return p_sum + scaled, q_sum + scaled * (off * inv_two)
 
-    p_sum, q_sum = lax.fori_loop(0, RT, finish, (nothing, nothing))
+    p_sum, q_sum = lax.fori_loop(0, RT, finish, (nothing, nothing), unroll=4)
+    rows_start(OUTER)
 
     def send_final():
+        columns_start(OUTER)
+
         def keep_final(g, _):
             block = S[pl.ds(pl.multiple_of(128 * g, 128), 128), :]
             fin_out[pl.ds(4 * g, 4)] = block.reshape(4, RT, CT).astype(BF16)
@@ -624,58 +709,78 @@
 
         lax.fori_loop(0, 16, keep_final, 0)
         move_tile(2, fin_out.at[lower_half], fin_in.at[lower_half], keeper)
+        move_tile(3, fin_out.at[upper_half], fin_in.at[upper_half], keeper)
         mirror_pack(1, S)
 
-    def send_final_rest():
-        move_tile(3, fin_out.at[upper_half], fin_in.at[upper_half], keeper)
-
-    totals = sums(4, to_message(p_sum, q_sum), send_final, send_final_rest)
+    def after_final():
+        corners_start(OUTER)
+        mirror_half(0, 0)
+        mirror_half(0, 1)
+        mirror_half(1, 0)
+        mirror_half(1, 1)
+        field_wait(SECOND)
+
+    totals = sums(4, to_message(p_sum, q_sum), send_final, after_final)
     p_two, q_two = from_message(totals / count)
 
-    def back_two(i):
-        normed = (second[i] - mean_two) * inv_two
-        scaled = outer[i] * gain_two
-        return valid_row(i) * inv_two * (scaled - p_two - normed * q_two)
-
-    keep_rows(GRAD_TWO, back_two)
-    halo_start(GRAD_TWO)
-    mirror_block(0)
-    grad_taps(1, ACTIVE, d_two, GRAD_TWO)
-    halo_wait(GRAD_TWO)
-    mirror_block(1)
-    spread(GRAD_TWO, d_two)
+    def grad_two(second, outer, valid):
+        normed = (second - mean_two) * inv_two
+        return valid * inv_two * (outer * gain_two - p_two - normed * q_two)
+
+    field_wait(OUTER)
+    spread(
+        GRAD_TWO,
+        d_two,
+        lambda e: grad_two(wide[SECOND, e], wide[OUTER, e], valid_wide(e)),
+        lambda side, g: grad_two(
+            beside_r[SECOND, side, g], beside_r[OUTER, side, g], valid_beside(side, g)
+        ),
+    )
     gain_one = gain_b[0]
 
     def descend(i, out, carry):
         p_sum, q_sum = carry
-        up_i = out * slope_one[i]
-        inner[i] = up_i
+        up_i = out * slope_one[EDGE + i]
+        wide[INNER, EDGE + i] = up_i
         scaled = up_i * gain_one
-        return p_sum + scaled, q_sum + scaled * ((first[i] - mean_one) * inv_one)
+        return p_sum + scaled, q_sum + scaled * ((wide[FIRST, EDGE + i] - mean_one) * inv_one)
 
     p_sum, q_sum = convolve(GRAD_TWO, d_two, 3, descend, (nothing, nothing))
+    rows_start(INNER)
+
+    def after_inner():
+        corners_start(INNER)
+        grad_taps_across(1)
 
     def beside_inner():
-        mirror_block(2)
-        grad_taps_across(1)
-
-    totals = sums(6, to_message(p_sum, q_sum), beside_inner, lambda: mirror_block(3))
+        columns_start(INNER)
+        grad_taps(1, ACTIVE, d_two, GRAD_TWO)
+
+    totals = sums(6, to_message(p_sum, q_sum), beside_inner, after_inner)
     p_one, q_one = from_message(totals / count)
 
-    def back_one(i):
-        normed = (first[i] - mean_one) * inv_one
-        scaled = inner[i] * gain_one
-        return valid_row(i) * inv_one * (scaled - p_one - normed * q_one)
-
-    keep_rows(GRAD_ONE, back_one)
-    halo_start(GRAD_ONE)
+    def grad_one(first, inner, valid):
+        normed = (first - mean_one) * inv_one
+        return valid * inv_one * (inner * gain_one - p_one - normed * q_one)
+
+    field_wait(INNER)
+    mirror_half(2, 0)
+    mirror_half(2, 1)
+    mirror_half(3, 0)
+    mirror_half(3, 1)
+    spread(
+        GRAD_ONE,
+        d_one,
+        lambda e: grad_one(wide[FIRST, e], wide[INNER, e], valid_wide(e)),
+        lambda side, g: grad_one(
+            beside_r[FIRST, side, g], beside_r[INNER, side, g], valid_beside(side, g)
+        ),
+    )
     grad_taps(0, PAIRS, d_one, GRAD_ONE)
     grad_taps_back(1)
-    halo_wait(GRAD_ONE)
-    spread(GRAD_ONE, d_one)
 
     def lower(i, out, carry):
-        S[pl.ds(i, CH, stride=RT), :] = (outer[i] + out) * valid_row(i)
+        S[pl.ds(i, CH, stride=RT), :] = (wide[OUTER, EDGE + i] + out) * valid_row(i)
         return carry
 
     convolve(GRAD_ONE, d_one, 1, lower, 0)
@@ -686,8 +791,9 @@
         return 0
 
     lax.fori_loop(0, 16, keep_grad, 0)
+    grad_taps_across(0)
     move_tile(4, gp_out.at[lower_half], gp_ref.at[lower_half], keeper)
-    grad_taps_across(0)
+    move_tile(5, gp_out.at[upper_half], gp_ref.at[upper_half], keeper)
     moved(2, fin_in.at[lower_half])
     moved(3, fin_in.at[upper_half])
     mirror_wait(1)
@@ -701,7 +807,6 @@
 
     lax.fori_loop(0, 16, join_final, 0)
     grad_taps_back(0)
-    move_tile(5, gp_out.at[upper_half], gp_ref.at[upper_half], keeper)
     grad_taps_end(1)
     grad_taps_end(0)
 
@@ -715,9 +820,9 @@
         size = G2 if q % 2 else G1
         wait_bytes(ar_r.at[q, pl.ds(0, size - 1)], ar_send_sem.at[q])
     for k in range(2):
-        wait_bytes(w_a.at[k, pl.ds(0, G1 - 1)], w_send_sem.at[k, 0])
-        wait_bytes(w_b.at[k, pl.ds(0, G2 - 1)], w_send_sem.at[k, 1])
-        wait_bytes(w_c.at[k, pl.ds(0, G1 - 1)], w_send_sem.at[k, 2])
+        wait_bytes(w_a.at[k, pl.ds(0, G2 - 1)], w_send_sem.at[k, 0])
+        wait_bytes(w_b.at[k, pl.ds(0, G1 - 1)], w_send_sem.at[k, 1])
+        wait_bytes(w_c.at[k, pl.ds(0, G2 - 1)], w_send_sem.at[k, 2])
     moved(4, gp_out.at[lower_half])
     moved(5, gp_out.at[upper_half])
 
@@ -728,12 +833,11 @@
     def per_device(pairs, w_first, w_second, gains, shifts, dilations, residue_count, cotangent):
         CH, RT, CT = pairs.shape
         G1, G2 = 2 * C, R // 2
-        G, share = max(G1, G2), 16 // G1
+        G, share = max(G1, G2), 16 // G2
         vmem = pl.BlockSpec(memory_space=pltpu.VMEM)
         smem = pl.BlockSpec(memory_space=pltpu.SMEM)
         anywhere = pl.BlockSpec(memory_space=pl.ANY)
         tile = pltpu.VMEM((CH, RT, CT), BF16)
-        field = pltpu.VMEM((RT, CH, CT), F32)
         flat = pltpu.VMEM((CH * RT, CT), F32)
         dma = pltpu.SemaphoreType.DMA
         return pl.pallas_call(
@@ -754,35 +858,34 @@
                 pltpu.VMEM((2, 4, 16, RT, CT), BF16),
                 pltpu.VMEM((2, 4, 16, RT, CT), BF16),
                 pltpu.VMEM((G2, 16, RT, CT), BF16),
-                pltpu.VMEM((4, RT + 2 * EDGE, CH, CT), BF16),
-                pltpu.VMEM((4, 2, 4, CH, CT), BF16),
-                pltpu.VMEM((4, 2, 8, CH, CT), BF16),
+                pltpu.VMEM((RT + 2 * EDGE, CH, CT), BF16),
+                pltpu.VMEM((2, 4, CH, CT), BF16),
+                pltpu.VMEM((2, 8, CH, CT), BF16),
                 pltpu.VMEM((4, RT + 2 * EDGE, 3 * CH, CT), BF16),
                 flat,
                 flat,
-                field,
-                field,
-                field,
-                field,
-                field,
+                pltpu.VMEM((4, RT + 2 * EDGE, CH, CT), F32),
+                pltpu.VMEM((4, 2, 4, CH, CT), F32),
+                pltpu.VMEM((4, 2, 8, CH, CT), F32),
+                pltpu.VMEM((RT + 2 * EDGE, CH, CT), F32),
                 pltpu.VMEM((4, CH, 9 * CH), BF16),
                 pltpu.VMEM((2, CH, CT), F32),
                 pltpu.VMEM((2, CH, CT), F32),
                 pltpu.VMEM((8, 1, CT), F32),
                 pltpu.VMEM((8, G, 1, CT), F32),
                 pltpu.VMEM((CH, 768), F32),
-                pltpu.VMEM((2, G1, share, 8, 384), F32),
+                pltpu.VMEM((2, G2, share, 8, 384), F32),
+                pltpu.VMEM((2, G2, share, 8, 384), F32),
+                pltpu.VMEM((2, share, 8, 384), F32),
                 pltpu.VMEM((2, G1, share, 8, 384), F32),
                 pltpu.VMEM((2, share, 8, 384), F32),
                 pltpu.VMEM((2, G2, share, 8, 384), F32),
-                pltpu.VMEM((2, share, 8, 384), F32),
-                pltpu.VMEM((2, G1, share, 8, 384), F32),
                 dma((6,)),
                 dma((6,)),
-                dma((4, 8)),
-                dma((4, 8)),
-                dma((2, 4)),
-                dma((2, 4)),
+                dma((5, 8)),
+                dma((5, 8)),
+                dma((2, 8)),
+                dma((2, 8)),
                 dma((8,)),
                 dma((8,)),
                 dma((G2,)),

time: 205 us -> 173 us (0.84)
  Pallas kernels: 199 us -> 167 us
    pallas_call x1, Pallas kernels: 199 us -> 167 us  [per_device(): pl.pallas_call(functools.partial(kernel, R, C), out_shape=(jax.ShapeDtype...]
where the time goes in v3:
time: 173 us; the launch traced here: 172 us
  Pallas kernels  167 us (97%)
  local copies, waits for them, and re-layouts  4 us (2%)
    pallas_call x1, Pallas kernels, per_device(): pl.pallas_call(functools.partial(kernel, R, C), out_shape=(jax.ShapeDtype...  167 us
    unnamed x7, local copies, waits for them, and re-layouts  4 us

profile of v3, /device:TPU:1, one launch (start us, length us, event | category | flops | bytes accessed | tf_op | source)
XLA Modules:
  0.0 171.8 jit_solution(3870385670533199346)
XLA Ops:
  1.3 166.5 %shard_map.103 = (bf16[64,32,128]{2,1,0:T(8,128)(2,1)}, bf16[64,32,128]{2,1,0:T(8,128)(2,1)}, f32[2,3,3,64,64]{4,3,2,1,0:T(8,128)}) custom-call(s32[2]{0:T(128)} %dil_ref.1, s32[1]{0:T(128)S(6)} %copy.14.count_ref, bf16[64,32,128]{2,1,0:T(8,128)(2,1)} %pairs_ref.1, bf16[64,32,128]{2,1,0:T(8,128)(2,1)} %cot_ref.1, bf16[3,3,64,64]{3,2,1,0:T(8,128)(2,1)} %w_first_ref.1, ...), custom_call_target="tpu_custom_call" | custom-call | flops 1811939328 | bytes 1048576 | tf_op jit(solution)/shard_map/pallas_call | solution.py:843
  167.8 0.0 copy-start.1
  167.8 1.9 %copy.15 = bf16[64,32,128]{2,1,0:T(8,128)(2,1)} copy(bf16[64,32,128]{2,1,0:T(8,128)(2,1)} %get-tuple-element.6) | data formatting | bytes 1048576
  169.8 0.0 copy-done.1
  169.8 0.0 copy-start
  169.8 0.8 copy.16
  170.6 0.5 copy-done
  171.0 0.8 copy.17
Async XLA Ops:
  167.8 1.9 %copy-start.1 = (bf16[64,32,128]{2,1,0:T(8,128)(2,1)S(1)}, bf16[64,32,128]{2,1,0:T(8,128)(2,1)}, u32[]{:S(2)}) copy-start(bf16[64,32,128]{2,1,0:T(8,128)(2,1)} %get-tuple-element.7) | copy-start | bytes 1572868
  169.8 1.3 copy-start

commit v4 on v3

--- a/solution.py
+++ b/solution.py
@@ -639,7 +639,7 @@
 
     def beside_first():
         columns_start(FIRST)
-        cross_on(0 * G2 // 16, 10 * G2 // 16)
+        cross_on(0, G2 // 2)
 
     mean_one, inv_one = norm(0, FIRST, total, beside_first, lambda: corners_start(FIRST))
     scale_one = inv_one * gain_b[0]
@@ -660,7 +660,7 @@
 
     field_wait(FIRST)
     spread(ACTIVE, d_two, active_row, active_beside)
-    cross_on(10 * G2 // 16, 16 * G2 // 16)
+    cross_on(G2 // 2, G2)
     total = convolve(ACTIVE, d_two, 2, keep(SECOND), nothing)
     rows_start(SECOND)
 

time: 173 us -> 172 us (level)
  no operation moved by 1% of the time
where the time goes in v4:
time: 172 us; the launch traced here: 171 us
  Pallas kernels  166 us (97%)
  local copies, waits for them, and re-layouts  4 us (2%)
    pallas_call x1, Pallas kernels, per_device(): pl.pallas_call(functools.partial(kernel, R, C), out_shape=(jax.ShapeDtype...  166 us
    unnamed x7, local copies, waits for them, and re-layouts  4 us

profile of v4, /device:TPU:1, one launch (start us, length us, event | category | flops | bytes accessed | tf_op | source)
XLA Modules:
  0.0 171.3 jit_solution(489369958617645016)
XLA Ops:
  1.3 166.0 %shard_map.103 = (bf16[64,32,128]{2,1,0:T(8,128)(2,1)}, bf16[64,32,128]{2,1,0:T(8,128)(2,1)}, f32[2,3,3,64,64]{4,3,2,1,0:T(8,128)}) custom-call(s32[2]{0:T(128)} %dil_ref.1, s32[1]{0:T(128)S(6)} %copy.14.count_ref, bf16[64,32,128]{2,1,0:T(8,128)(2,1)} %pairs_ref.1, bf16[64,32,128]{2,1,0:T(8,128)(2,1)} %cot_ref.1, bf16[3,3,64,64]{3,2,1,0:T(8,128)(2,1)} %w_first_ref.1, ...), custom_call_target="tpu_custom_call" | custom-call | flops 1811939328 | bytes 1048576 | tf_op jit(solution)/shard_map/pallas_call | solution.py:843
  167.3 0.0 copy-start.1
  167.3 1.9 %copy.15 = bf16[64,32,128]{2,1,0:T(8,128)(2,1)} copy(bf16[64,32,128]{2,1,0:T(8,128)(2,1)} %get-tuple-element.6) | data formatting | bytes 1048576
  169.2 0.0 copy-done.1
  169.2 0.0 copy-start
  169.2 0.8 copy.16
  170.0 0.5 copy-done
  170.4 0.8 copy.17
Async XLA Ops:
  167.3 1.9 %copy-start.1 = (bf16[64,32,128]{2,1,0:T(8,128)(2,1)S(1)}, bf16[64,32,128]{2,1,0:T(8,128)(2,1)}, u32[]{:S(2)}) copy-start(bf16[64,32,128]{2,1,0:T(8,128)(2,1)} %get-tuple-element.7) | copy-start | bytes 1572868
  169.2 1.3 copy-start
